TPU v7x, 512 devices: a whole 4x8x8 slice. The times are simulated.
512 devices in a mesh: dp: 32 (over z, y_lo, core), tensor: 16 (over y_hi, x).
Axes of the slice: x: 4, y: 8 (y_hi: 4, y_lo: 2; y = y_hi * 2 + y_lo), z: 8, core: 2. Of those that a mesh axis runs over, the one named last changes fastest.
Arguments:
- hidden: bfloat16 [16384, 24576], P('dp', 'tensor'), may hold values from -6 to 6
- resid: bfloat16 [16384, 3072], P(('dp', 'tensor')), may hold values from -6 to 6
- down_w: bfloat16 [24576, 3072], P('tensor', 'dp'), may hold values from -0.0390625 to 0.0390625
- inputs: bfloat16 [16384, 1024], P('dp'), may hold values from -6 to 6
- gain: float32 [1024], replicated, may hold values from 0.25 to 1.75
- head: bfloat16 [1024, 3072], P(None, 'tensor'), may hold values from -0.1875 to 0.1875
Outputs:
- input_grad: bfloat16 [16384, 1024], P(('dp', 'tensor'))
- head_grad: float32 [1024, 3072], P(None, 'tensor')
All inputs are finite; a program needn't handle non-finite values.
Results may differ from a plain program's by a relative error of at most 0.027.
Values may be sent and summed in bfloat16 or wider, within the bound.
No kernel may reach another device: no remote copies, remote signals or barrier semaphores. Data moves between devices by JAX's collectives and lax.ppermute only.
A program may use at most 64 MiB of HBM per device.

v0:
```python
import jax
import jax.numpy as jnp
from jax import lax
from jax.sharding import PartitionSpec as P


def local(hidden, resid, down_w, inputs, gain, head):
    tok_rows = hidden.shape[0]
    shards = lax.axis_size("tensor")
    mine = lax.axis_index("tensor")
    partial_value = jnp.dot(
        hidden, lax.all_gather(down_w, "dp", axis=1, tiled=True), preferred_element_type=jnp.float32
    )
    summed = lax.psum_scatter(
        partial_value.astype(jnp.bfloat16), "tensor", scatter_dimension=0, tiled=True
    ).astype(jnp.float32)
    features = resid.astype(jnp.float32) + summed
    center = features - jnp.mean(features, axis=1, keepdims=True)
    variance = jnp.mean(center * center, axis=1, keepdims=True)
    target = (center * lax.rsqrt(variance + 1e-06)).astype(jnp.bfloat16)
    whole = lax.all_gather(target, "tensor", axis=0, tiled=True)
    width = whole.shape[1] // shards
    target_cols = lax.dynamic_slice_in_dim(whole, mine * width, width, 1)
    values = inputs.astype(jnp.float32)
    rms = jnp.sqrt(jnp.mean(values * values, axis=1, keepdims=True) + 1e-06)
    normed = (values / rms * gain).astype(jnp.bfloat16)
    pred = jnp.dot(normed, head, preferred_element_type=jnp.float32)
    delta = (pred - target_cols.astype(jnp.float32)).astype(jnp.bfloat16)
    local_grad = lax.dot_general(
        normed, delta, (((0,), (0,)), ((), ())), preferred_element_type=jnp.float32
    )
    head_grad = lax.psum(local_grad.astype(jnp.bfloat16), "dp").astype(jnp.float32) / tok_rows
    own_rows = tok_rows // shards
    dnormed = lax.psum_scatter(
        lax.dot_general(
            delta, head, (((1,), (1,)), ((), ())), preferred_element_type=jnp.float32
        ).astype(jnp.bfloat16),
        "tensor",
        scatter_dimension=0,
        tiled=True,
    ).astype(jnp.float32)
    own_values = lax.dynamic_slice_in_dim(values, mine * own_rows, own_rows, 0)
    own_rms = lax.dynamic_slice_in_dim(rms, mine * own_rows, own_rows, 0)
    scaled = gain * dnormed
    total = jnp.sum(scaled * own_values, axis=1, keepdims=True)
    width_in = values.shape[1]
    input_grad = scaled / own_rms - own_values * total / (width_in * own_rms * own_rms * own_rms)
    return (input_grad.astype(jnp.bfloat16), head_grad)


def solution(mesh):
    in_specs = (
        P("dp", "tensor"),
        P(("dp", "tensor"), None),
        P("tensor", "dp"),
        P("dp", None),
        P(),
        P(None, "tensor"),
    )
    out_specs = (P(("dp", "tensor"), None), P(None, "tensor"))
    return jax.shard_map(local, mesh=mesh, in_specs=in_specs, out_specs=out_specs, check_vma=False)
```

profile of v0, /device:TPU:1, one launch (start us, length us, event | category | flops | bytes accessed | tf_op | source)
XLA Modules:
  0.0 600.2 jit_solution(4752613159202793303)
XLA Ops:
  7.2 0.0 copy-start
  7.2 0.0 all-gather.3.cloned.1.call-start
  7.2 0.7 all-gather.3.cloned.1.call-update
  7.9 0.0 reduce-scatter.7.cloned.1.call-start
  8.0 84.6 %all-gather.3.cloned.1.call-done = bf16[1536,3072]{0,1:T(8,128)(2,1)} async-done(((bf16[1536,96]{0,1:T(8,128)(2,1)}), bf16[1536,3072]{0,1:T(8,128)(2,1)}) %all-gather.3.cloned.1.call-update) | async-done | bytes 9437200 | tf_op jit(solution)/shard_map/all_gather | solution.py:12
  92.6 0.0 copy-done
  92.6 10.1 %convolution_convert_fusion = bf16[512,3072]{1,0:T(8,128)(2,1)} fusion(bf16[512,1536]{1,0:T(8,128)(2,1)S(1)} %copy-done, bf16[1536,3072]{0,1:T(8,128)(2,1)} %all-gather.3.cloned.1.call-done), kind=kOutput, calls=%fused_computation | convolution fusion | flops 4833411072 | bytes 14155776 | tf_op jit(solution)/shard_map/dot_general | solution.py:11
  102.7 0.0 copy-start.3
  102.7 0.0 copy-start.1
  102.7 0.0 reduce-scatter.7.cloned.1.call-update
  102.7 0.0 copy-start.5
  102.7 0.0 all-gather.5.cloned.1.call-start
  102.8 93.5 %reduce-scatter.7.cloned.1.call-done = bf16[32,3072]{1,0:T(8,128)(2,1)} async-done(((bf16[512,3072]{1,0:T(8,128)(2,1)}), bf16[32,3072]{1,0:T(8,128)(2,1)}) %reduce-scatter.7.cloned.1.call-update) | async-done | bytes 196624 | tf_op jit(solution)/shard_map/reduce_scatter | solution.py:14
  196.3 0.0 copy-done.3
  196.3 1.1 fusion.2
  197.4 1.1 multiply_reduce_fusion.1
  198.5 1.7 multiply_convert_fusion.1
  200.2 0.0 all-gather.5.cloned.1.call-update
  200.3 0.0 copy-start.4
  200.3 0.0 all-reduce.2.cloned.1.call-start
  200.3 0.0 copy-done.1
  200.3 0.3 multiply_reduce_fusion
  200.6 0.0 copy-done.5
  200.6 1.4 multiply_convert_fusion
  202.0 71.2 %all-gather.5.cloned.1.call-done = bf16[512,3072]{1,0:T(8,128)(2,1)} async-done(((bf16[32,3072]{1,0:T(8,128)(2,1)}), bf16[512,3072]{1,0:T(8,128)(2,1)}) %all-gather.5.cloned.1.call-update) | async-done | bytes 3145744 | tf_op jit(solution)/shard_map/all_gather | solution.py:21
  273.3 1.1 constant_dynamic-slice_fusion
  274.4 0.1 copy.19
  274.5 0.0 copy-done.4
  274.6 0.0 copy-start.2
  274.6 1.8 fusion
  276.4 0.0 copy-done.2
  276.4 1.1 convolution_convert_fusion.2
  277.5 0.0 all-reduce.2.cloned.1.call-update
  277.6 0.0 reduce-scatter.5.cloned.1.call-start
  277.6 1.5 convolution_convert_fusion.1
  279.1 0.0 reduce-scatter.5.cloned.1.call-update
  279.1 1.6 convert_element_type.39
  280.7 0.1 fusion.3
  280.8 213.5 %all-reduce.2.cloned.1.call-done = bf16[1024,192]{0,1:T(8,128)(2,1)} async-done(((bf16[1024,192]{0,1:T(8,128)(2,1)}), bf16[1024,192]{0,1:T(8,128)(2,1)}) %all-reduce.2.cloned.1.call-update) | async-done | bytes 393232 | tf_op jit(solution)/shard_map/psum | solution.py:32
  494.2 2.0 convert_multiply_fusion
  496.2 94.7 %reduce-scatter.5.cloned.1.call-done = bf16[32,1024]{1,0:T(8,128)(2,1)} async-done(((bf16[512,1024]{1,0:T(8,128)(2,1)}), bf16[32,1024]{1,0:T(8,128)(2,1)}) %reduce-scatter.5.cloned.1.call-update) | async-done | bytes 65552 | tf_op jit(solution)/shard_map/reduce_scatter | solution.py:34
  590.9 1.1 multiply_reduce_fusion.2
  592.0 1.7 subtract_convert_fusion
  (3 shorter events, 0.0 us)
Async XLA Ops:
  7.2 85.4 %copy-start = (bf16[512,1536]{1,0:T(8,128)(2,1)S(1)}, bf16[512,1536]{1,0:T(8,128)(2,1)}, u32[]{:S(2)}) copy-start(bf16[512,1536]{1,0:T(8,128)(2,1)} %param.6) | copy-start | bytes 4718596
  7.2 85.4 %all-gather.3.cloned.1.call-start = ((), (), s32[]{:S(2)}) async-start(), calls=%async_computation.2 | async-start | bytes 9732096 | tf_op jit(solution)/shard_map/all_gather | solution.py:12
  7.9 188.4 %reduce-scatter.7.cloned.1.call-start = ((), (), s32[]{:S(2)}) async-start(), calls=%async_computation.6 | async-start | bytes 3342336 | tf_op jit(solution)/shard_map/reduce_scatter | solution.py:14
  102.7 93.6 %copy-start.3 = (bf16[32,3072]{1,0:T(8,128)(2,1)S(1)}, bf16[32,3072]{1,0:T(8,128)(2,1)}, u32[]{:S(2)}) copy-start(bf16[32,3072]{1,0:T(8,128)(2,1)} %param.7) | copy-start | bytes 589828
  102.7 97.7 %copy-start.1 = (bf16[512,1024]{1,0:T(8,128)(2,1)S(1)}, bf16[512,1024]{1,0:T(8,128)(2,1)}, u32[]{:S(2)}) copy-start(bf16[512,1024]{1,0:T(8,128)(2,1)} %param.9) | copy-start | bytes 3145732
  102.7 97.9 %copy-start.5 = (f32[1024]{0:T(1024)S(1)}, f32[1024]{0:T(1024)}, u32[]{:S(2)}) copy-start(f32[1024]{0:T(1024)} %param.10) | copy-start | bytes 12292
  102.7 170.6 %all-gather.5.cloned.1.call-start = ((), (), s32[]{:S(2)}) async-start(), calls=%async_computation.3 | async-start | bytes 3342336 | tf_op jit(solution)/shard_map/all_gather | solution.py:21
  200.3 74.3 %copy-start.4 = (bf16[1024,192]{0,1:T(8,128)(2,1)S(1)}, bf16[1024,192]{0,1:T(8,128)(2,1)}, u32[]{:S(2)}) copy-start(bf16[1024,192]{0,1:T(8,128)(2,1)} %param.11) | copy-start | bytes 1179652
  200.3 293.9 %all-reduce.2.cloned.1.call-start = ((), (), s32[]{:S(2)}) async-start(), calls=%async_computation.5 | async-start | bytes 786432 | tf_op jit(solution)/shard_map/psum | solution.py:32
  274.6 1.8 copy-start.2
  277.6 313.3 %reduce-scatter.5.cloned.1.call-start = ((), (), s32[]{:S(2)}) async-start(), calls=%async_computation.4 | async-start | bytes 1114112 | tf_op jit(solution)/shard_map/reduce_scatter | solution.py:34
Sparse Core Ops, SparseCore 0:
  10.2 82.3 all-gather.2
  102.8 93.4 reduce-scatter.6
  200.4 72.8 all-gather.4
  277.7 216.4 all-reduce.1
  498.7 92.1 reduce-scatter.4
where the time goes:
time: 601 us; the launch traced here: 600 us
  waiting for transfers between devices  558 us (93%)
  matrix products  14.5 us (2%)
  between operations  13.9 us (2%)
  other arithmetic  12 us (2%)
    psum x1, waiting for transfers between devices, local(): lax.psum(local_grad.astype(jnp.bfloat16), 'dp').astype(jnp.float32)  213 us
    reduce_scatter x1, waiting for transfers between devices, local(): lax.psum_scatter(lax.dot_general(delta, head, (((1,), (1,)), ((), ())), p...  94.7 us
    reduce_scatter x1, waiting for transfers between devices, local(): lax.psum_scatter(partial_value.astype(jnp.bfloat16), 'tensor', scatter_di...  93.5 us
    all_gather x1, waiting for transfers between devices, local(): lax.all_gather(down_w, 'dp', axis=1, tiled=True)  84.6 us
    all_gather x1, waiting for transfers between devices, local(): whole = lax.all_gather(target, 'tensor', axis=0, tiled=True)  71.2 us
  transfers between devices with their start and end apart: 5, of which 5 were waited for; matrix products, arithmetic and copies ran while one was open for 1% of the time, Pallas kernels for 0%

commit v1 on v0

v1 whole, which is shorter than its diff:
```python
import jax
import jax.numpy as jnp
from jax import lax
from jax.sharding import Mesh, PartitionSpec as P

AXES = ("z", "yl", "c", "yh", "x")
SIZES = (8, 2, 2, 4, 4)
TENSOR = ("yh", "x")
SWAP = [(0, 1), (1, 0)]
F32 = jnp.float32
BF16 = jnp.bfloat16


def dot_nt(a, b):
    return lax.dot_general(a, b, (((1,), (1,)), ((), ())), preferred_element_type=F32)


def local(hidden, resid, down_w, inputs, gain, head):
    rows, depth = hidden.shape
    half = down_w.shape[1]
    width = inputs.shape[1]
    nz, nyh, nx = 8, 4, 4
    nt = nyh * nx
    own = rows // nt
    cols = nz * half
    yl = lax.axis_index("yl")
    core = lax.axis_index("c")
    mine = lax.axis_index(TENSOR)

    w = lax.all_gather(down_w.T, "z", axis=0, tiled=True)

    hidden_y = lax.ppermute(hidden, "yl", SWAP)
    hidden_c = lax.ppermute(hidden, "c", SWAP)
    hidden_yc = lax.ppermute(hidden_y, "c", SWAP)

    inputs_c = lax.ppermute(inputs, "c", SWAP)

    def norm(block):
        values = block.astype(F32)
        rms = jnp.sqrt(jnp.mean(values * values, axis=1, keepdims=True) + 1e-06)
        return (values / rms * gain).astype(BF16)

    def rows_of(block):
        return lax.dynamic_slice_in_dim(block, mine * own, own, 0)

    normed = norm(inputs)
    normed_c = norm(inputs_c)
    normed_own = jnp.concatenate([rows_of(normed), rows_of(normed_c)], axis=0)
    head_half = lax.dynamic_slice_in_dim(head.T, core * half, half, 0)
    head_y = lax.all_gather(head_half, "yh", axis=0)
    head_x = lax.all_to_all(
        jnp.broadcast_to(head_y[None], (nx,) + head_y.shape), "x", 0, 0, tiled=True
    )
    head_all = head_x.reshape(2, 2, nyh, half, width).transpose(1, 2, 0, 3, 4).reshape(2, cols, width)
    pred = jnp.stack([dot_nt(normed_own, head_all[0]), dot_nt(normed_own, head_all[1])])

    resid_parts = resid.reshape(own, nz, 2, 2, half)
    resid_keep = lax.dynamic_index_in_dim(resid_parts, core, 3, keepdims=False)
    resid_send = lax.dynamic_index_in_dim(resid_parts, 1 - core, 3, keepdims=False)
    resid_recv = lax.ppermute(resid_send, "c", SWAP)
    resid_own = jnp.stack([resid_keep, resid_recv]).transpose(3, 0, 1, 2, 4).reshape(2, 2 * own, cols)

    def partial(block):
        return dot_nt(block, w).astype(BF16).reshape(nyh, nx, own, cols)

    parts = jnp.stack(
        [
            jnp.stack([partial(hidden), partial(hidden_c)]),
            jnp.stack([partial(hidden_y), partial(hidden_yc)]),
        ]
    )
    parts = parts.transpose(3, 0, 2, 1, 4, 5)
    got_x = lax.all_to_all(parts, "x", 0, 0, tiled=True)
    sum_x = jnp.sum(got_x.astype(F32), axis=0).astype(BF16)
    sum_x = jnp.where(yl == 0, sum_x, sum_x[::-1])
    send_y = sum_x.transpose(1, 0, 2, 3, 4).reshape(2 * nyh, 2 * own, cols)
    got_y = lax.all_to_all(send_y, ("yh", "yl"), 0, 0, tiled=True)
    feats = jnp.sum(got_y.reshape(nyh, 2, 2 * own, cols).astype(F32), axis=0)
    feats = feats + resid_own.astype(F32)

    count = 2 * cols
    mean = jnp.mean(feats, axis=(0, 2))
    square = jnp.sum((feats - mean[None, :, None]) ** 2, axis=(0, 2))
    stats = jnp.stack([mean, square]).reshape(2, 2, own)
    other = lax.ppermute(stats, "c", SWAP)[:, ::-1].reshape(2, 2 * own)
    gap = mean - other[0]
    total_mean = 0.5 * (mean + other[0])
    variance = (square + other[1] + gap * gap * (0.5 * count)) / (2 * count)
    scale = lax.rsqrt(variance + 1e-06)
    target = ((feats - total_mean[None, :, None]) * scale[None, :, None]).astype(BF16)
    delta = (pred - target.astype(F32)).astype(BF16)

    send_t = delta.reshape(2, 2 * own, nz, half).transpose(2, 0, 1, 3).reshape(nt, 2 * own, half)
    got_t = lax.all_to_all(send_t, TENSOR, 0, 0, tiled=True)

    def grad(block, delta_rows):
        return lax.dot_general(
            block, delta_rows.reshape(rows, half), (((0,), (0,)), ((), ())), preferred_element_type=F32
        )

    head_part = (grad(normed, got_t[:, :own]) + grad(normed_c, got_t[:, own:])).astype(BF16)
    head_rows = width // (2 * nz)
    got_g = lax.all_to_all(head_part.reshape(2 * nz, head_rows, half), ("z", "yl"), 0, 0, tiled=True)
    head_sum = jnp.sum(got_g.astype(F32), axis=0).astype(BF16)
    all_g = lax.all_to_all(
        jnp.broadcast_to(head_sum[None], (2 * nz, head_rows, half)), ("z", "yl"), 0, 0, tiled=True
    ).reshape(width, half)
    other_g = lax.ppermute(all_g, "c", SWAP)
    left = jnp.where(core == 0, all_g, other_g)
    right = jnp.where(core == 0, other_g, all_g)
    head_grad = jnp.concatenate([left, right], axis=1).astype(F32) / rows

    dn = lax.dot_general(
        delta[0], head_all[0], (((1,), (0,)), ((), ())), preferred_element_type=F32
    ) + lax.dot_general(delta[1], head_all[1], (((1,), (0,)), ((), ())), preferred_element_type=F32)
    dnormed = dn[:own] + lax.ppermute(dn[own:].astype(BF16), "c", SWAP).astype(F32)
    values = rows_of(inputs).astype(F32)
    rms = jnp.sqrt(jnp.mean(values * values, axis=1, keepdims=True) + 1e-06)
    scaled = gain * dnormed
    total = jnp.sum(scaled * values, axis=1, keepdims=True)
    input_grad = scaled / rms - values * total / (width * rms * rms * rms)
    return input_grad.astype(BF16), head_grad


def solution(mesh):
    fine = Mesh(mesh.devices.reshape(SIZES), AXES)
    dp, tensor = ("z", "yl", "c"), ("yh", "x")
    in_specs = (P(dp, tensor), P(dp + tensor, None), P(tensor, dp), P(dp, None), P(), P(None, tensor))
    out_specs = (P(dp + tensor, None), P(None, tensor))
    return jax.shard_map(local, mesh=fine, in_specs=in_specs, out_specs=out_specs, check_vma=False)
```

time: 601 us -> 275 us (0.46)
  waiting for transfers between devices: 558 us -> 87.8 us
  starting transfers between devices: 0.2 us -> 73.8 us
  local copies, waits for them, and re-layouts: 1.29 us -> 34.5 us
  blocking collectives: 0 us -> 20.5 us
  other arithmetic: 12 us -> 25.4 us
    psum x1 -> x0, waiting for transfers between devices: 213 us -> none  [local(): lax.psum(local_grad.astype(jnp.bfloat16), 'dp').astype(jnp.float32)]
    reduce_scatter x2 -> x0, waiting for transfers between devices: 188 us -> none  [the longest x1 94.7 us: local(): lax.psum_scatter(lax.dot_general(delta, head, (((1,), (1,)), ((), ())), p...]
    all_gather x2 -> x1, waiting for transfers between devices: 156 us -> 6.04 us  [local(): w = lax.all_gather(down_w.T, 'z', axis=0, tiled=True)]
    all_to_all x0 -> x6, waiting for transfers between devices: none -> 50.9 us  [the longest x1 12.9 us: local(): got_x = lax.all_to_all(parts, 'x', 0, 0, tiled=True)]
    ppermute x0 -> x8, starting transfers between devices: none -> 41.2 us  [the longest x1 8.76 us: local(): other = lax.ppermute(stats, 'c', SWAP)[:, ::-1].reshape(2, 2 * own)]
    all_to_all x0 -> x6, starting transfers between devices: none -> 32.6 us  [the longest x1 7.92 us: local(): lax.all_to_all(head_part.reshape(2 * nz, head_rows, half), ('z', 'yl'), 0...]
    ppermute x0 -> x8, waiting for transfers between devices: none -> 30.2 us  [the longest x1 29.5 us: local(): hidden_y = lax.ppermute(hidden, 'yl', SWAP)]
    all_gather x0 -> x1, blocking collectives: none -> 20.5 us  [local(): head_y = lax.all_gather(head_half, 'yh', axis=0)]
  transfers between devices with their start and end apart: 5 -> 15, of which waited for: 5 -> 9; matrix products, arithmetic and copies ran while one was open for 1% -> 18% of each run, Pallas kernels for 0% -> 0%
where the time goes in v1:
time: 275 us; the launch traced here: 274 us
  waiting for transfers between devices  87.8 us (32%)
  starting transfers between devices  73.8 us (27%)
  local copies, waits for them, and re-layouts  34.5 us (13%)
  other arithmetic  25.4 us (9%)
  blocking collectives  20.5 us (7%)
  matrix products  17.2 us (6%)
  between operations  14.5 us (5%)
    ppermute x1, waiting for transfers between devices, local(): hidden_y = lax.ppermute(hidden, 'yl', SWAP)  29.5 us
    all_gather x1, blocking collectives, local(): head_y = lax.all_gather(head_half, 'yh', axis=0)  20.5 us
    all_to_all x1, waiting for transfers between devices, local(): got_x = lax.all_to_all(parts, 'x', 0, 0, tiled=True)  12.9 us
    dot_general x6, matrix products, dot_nt(): lax.dot_general(a, b, (((1,), (1,)), ((), ())), preferred_element_type=F32)  12.8 us
    all_to_all x1, waiting for transfers between devices, local(): got_y = lax.all_to_all(send_y, ('yh', 'yl'), 0, 0, tiled=True)  10.1 us
    all_to_all x1, waiting for transfers between devices, local(): lax.all_to_all(jnp.broadcast_to(head_y[None], (nx,) + head_y.shape), 'x',...  9.21 us
    ppermute x1, starting transfers between devices, local(): other = lax.ppermute(stats, 'c', SWAP)[:, ::-1].reshape(2, 2 * own)  8.76 us
    ppermute x1, starting transfers between devices, local(): hidden_yc = lax.ppermute(hidden_y, 'c', SWAP)  7.95 us
  transfers between devices with their start and end apart: 15, of which 9 were waited for; matrix products, arithmetic and copies ran while one was open for 18% of the time, Pallas kernels for 0%

profile of v1, /device:TPU:1, one launch (start us, length us, event | category | flops | bytes accessed | tf_op | source)
XLA Modules:
  0.0 273.7 jit_solution(8315403905843608532)
XLA Ops:
  7.9 4.2 %collective-permute-start.2 = (bf16[512,1536]{1,0:T(8,128)(2,1)}, bf16[512,1536]{1,0:T(8,128)(2,1)S(1)}, u32[]{:S(2)}, u32[]{:S(2)}) collective-permute-start(bf16[512,1536]{1,0:T(8,128)(2,1)} %param.6), channel_id=1, source_target_pairs={{0,32},{32,0},{1,33},{33,1},{2,34},{34,2},{3,35},{35,3},{4,36},{36... | collective-permute-start | bytes 4718600 | tf_op jit(solution)/shard_map/ppermute | solution.py:32
  12.1 29.5 %collective-permute-done.2 = bf16[512,1536]{1,0:T(8,128)(2,1)S(1)} collective-permute-done((bf16[512,1536]{1,0:T(8,128)(2,1)}, bf16[512,1536]{1,0:T(8,128)(2,1)S(1)}, u32[]{:S(2)}, u32[]{:S(2)}) %collective-permute-start.2) | collective-permute-done | bytes 1572896 | tf_op jit(solution)/shard_map/ppermute | solution.py:32
  41.6 7.9 %collective-permute-start.3 = (bf16[512,1536]{1,0:T(8,128)(2,1)S(1)}, bf16[512,1536]{1,0:T(8,128)(2,1)}, u32[]{:S(2)}, u32[]{:S(2)}) collective-permute-start(bf16[512,1536]{1,0:T(8,128)(2,1)S(1)} %collective-permute-done.2), channel_id=1, source_target_pairs={{0,16},{16,0},{1,17},{17,1},{2,18},{18,2},{3,19},{19,3},{4,20},{20... | collective-permute-start | bytes 4718600 | tf_op jit(solution)/shard_map/ppermute | solution.py:34
  49.5 1.9 collective-permute-start.1
  51.5 6.0 %all-gather.3.cloned.1.call-done = bf16[768,1536]{1,0:T(8,128)(2,1)} async-done(((bf16[96,1536]{1,0:T(8,128)(2,1)}), bf16[768,1536]{1,0:T(8,128)(2,1)}) %all-gather.3.cloned.1.call-update) | async-done | bytes 2359312 | tf_op jit(solution)/shard_map/all_gather | solution.py:30
  57.5 3.2 %convolution_convert_fusion.1 = bf16[512,768]{1,0:T(8,128)(2,1)S(1)} fusion(bf16[512,1536]{1,0:T(8,128)(2,1)S(1)} %collective-permute-done.2, bf16[768,1536]{1,0:T(8,128)(2,1)} %all-gather.3.cloned.1.call-done), kind=kOutput, calls=%fused_computation.17 | convolution fusion | flops 1208352768 | bytes 4718592 | tf_op jit(solution)/shard_map/dot_general | solution.py:15
  62.2 2.8 %convolution_convert_fusion = bf16[512,768]{1,0:T(8,128)(2,1)S(1)} fusion(bf16[512,1536]{1,0:T(8,128)(2,1)} %collective-permute-done.3, bf16[768,1536]{1,0:T(8,128)(2,1)S(1)} %copy-done.13), kind=kOutput, calls=%fused_computation.16 | convolution fusion | flops 1208352768 | bytes 4718592 | tf_op jit(solution)/shard_map/dot_general | solution.py:15
  65.0 2.8 %convolution_convert_fusion.2 = bf16[512,768]{1,0:T(8,128)(2,1)S(1)} fusion(bf16[512,1536]{1,0:T(8,128)(2,1)} %collective-permute-done.1, bf16[768,1536]{1,0:T(8,128)(2,1)S(1)} %copy-done.13), kind=kOutput, calls=%fused_computation.18 | convolution fusion | flops 1208352768 | bytes 4718592 | tf_op jit(solution)/shard_map/dot_general | solution.py:15
  68.1 1.9 maximum_bitcast_fusion
  70.1 4.0 %all-to-all-start.1 = ((bf16[4,2,4,2,32,768]{5,4,2,3,1,0:T(8,128)(2,1)}), bf16[4,2,4,2,32,768]{5,4,2,3,1,0:T(8,128)(2,1)S(1)}, u32[]{:S(2)}, u32[]{:S(2)}) async-start(bf16[4,2,4,2,32,768]{5,4,2,3,1,0:T(8,128)(2,1)} %maximum_bitcast_fusion), calls=%async_computation.1 | async-start | bytes 6291456 | tf_op jit(solution)/shard_map/all_to_all | solution.py:73
  74.1 20.5 %all-gather = bf16[384,1024]{1,0:T(8,128)(2,1)} all-gather(bf16[96,1024]{1,0:T(8,128)(2,1)S(1)} %dynamic-slice_bitcast_fusion), channel_id=2, replica_groups=mesh['z'=8,'yl'=2,'c'=2,'yh'=4,'x'=4] {'yh'}, dimensions={0}, use_global_device_ids=true | all-gather | bytes 983040 | tf_op jit(solution)/shard_map/all_gather | solution.py:50
  94.6 12.9 %all-to-all-done.1 = bf16[4,2,4,2,32,768]{5,4,2,3,1,0:T(8,128)(2,1)S(1)} async-done(((bf16[4,2,4,2,32,768]{5,4,2,3,1,0:T(8,128)(2,1)}), bf16[4,2,4,2,32,768]{5,4,2,3,1,0:T(8,128)(2,1)S(1)}, u32[]{:S(2)}, u32[]{:S(2)}) %all-to-all-start.1) | async-done | bytes 3145760 | tf_op jit(solution)/shard_map/all_to_all | solution.py:73
  107.5 3.2 %broadcast_in_dim.4 = bf16[4,4,96,1024]{3,2,1,0:T(8,128)(2,1)} broadcast(bf16[4,96,1024]{2,1,0:T(8,128)(2,1)} %bitcast.91), dimensions={1,2,3} | broadcast | bytes 3932160 | tf_op jit(solution)/shard_map/broadcast_in_dim | solution.py:52
  110.7 4.6 %all-to-all-start = ((bf16[4,4,96,1024]{3,2,1,0:T(8,128)(2,1)}), bf16[4,4,96,1024]{3,2,1,0:T(8,128)(2,1)}, u32[]{:S(2)}, u32[]{:S(2)}) async-start(bf16[4,4,96,1024]{3,2,1,0:T(8,128)(2,1)} %broadcast_in_dim.4), calls=%async_computation | async-start | bytes 6291456 | tf_op jit(solution)/shard_map/all_to_all | solution.py:51
  115.3 7.0 %collective-permute-start = (bf16[512,1024]{1,0:T(8,128)(2,1)}, bf16[512,1024]{1,0:T(8,128)(2,1)}, u32[]{:S(2)}, u32[]{:S(2)}) collective-permute-start(bf16[512,1024]{1,0:T(8,128)(2,1)} %param.9), channel_id=1, source_target_pairs={{0,16},{16,0},{1,17},{17,1},{2,18},{18,2},{3,19},{19,3},{4,20},{20... | collective-permute-start | bytes 3145736 | tf_op jit(solution)/shard_map/ppermute | solution.py:36
  122.3 1.9 reshape.156
  124.2 1.7 constant_dynamic-slice_fusion.1
  126.6 1.9 collective-permute-start.4
  134.4 1.7 reduce_sum.95
  136.1 1.6 fusion.7
  138.7 9.2 %all-to-all-done = bf16[4,4,96,1024]{3,2,1,0:T(8,128)(2,1)} async-done(((bf16[4,4,96,1024]{3,2,1,0:T(8,128)(2,1)}), bf16[4,4,96,1024]{3,2,1,0:T(8,128)(2,1)}, u32[]{:S(2)}, u32[]{:S(2)}) %all-to-all-start) | async-done | bytes 3145760 | tf_op jit(solution)/shard_map/all_to_all | solution.py:51
  147.9 6.4 %all-to-all-start.2 = ((bf16[8,64,768]{2,1,0:T(8,128)(2,1)}), bf16[8,64,768]{2,1,0:T(8,128)(2,1)}, u32[]{:S(2)}, u32[]{:S(2)}) async-start(bf16[8,64,768]{2,1,0:T(8,128)(2,1)} %bitcast.18), calls=%async_computation.2 | async-start | bytes 1572864 | tf_op jit(solution)/shard_map/all_to_all | solution.py:77
  154.4 2.1 fusion.2
  157.8 2.3 fusion.27
  161.8 10.1 %all-to-all-done.2 = bf16[8,64,768]{2,1,0:T(8,128)(2,1)} async-done(((bf16[8,64,768]{2,1,0:T(8,128)(2,1)}), bf16[8,64,768]{2,1,0:T(8,128)(2,1)}, u32[]{:S(2)}, u32[]{:S(2)}) %all-to-all-start.2) | async-done | bytes 786464 | tf_op jit(solution)/shard_map/all_to_all | solution.py:77
  171.9 2.0 convert_reduce_fusion
  173.9 2.0 reduce_sum.97
  177.4 1.9 multiply_reduce_fusion
  179.9 8.8 %collective-permute-start.5 = (f32[2,2,32]{2,1,0:T(2,128)}, f32[2,2,32]{2,1,0:T(2,128)S(1)}, u32[]{:S(2)}, u32[]{:S(2)}) collective-permute-start(f32[2,2,32]{2,1,0:T(2,128)} %pad_maximum_fusion.5), channel_id=1, source_target_pairs={{0,16},{16,0},{1,17},{17,1},{2,18},{18,2},{3,19},{19,3},{4,20},{20... | collective-permute-start | bytes 1544 | tf_op jit(solution)/shard_map/ppermute | solution.py:85
  190.0 1.8 stack.59
  191.7 1.7 copy.38
  193.4 1.8 stack.60
  195.2 1.7 copy.39
  198.1 2.0 reduce_sum.103
  201.6 2.3 fusion.8
  203.9 4.2 %all-to-all-start.3 = ((bf16[16,64,96]{2,1,0:T(8,128)(2,1)}), bf16[16,64,96]{2,1,0:T(8,128)(2,1)}, u32[]{:S(2)}, u32[]{:S(2)}) async-start(bf16[16,64,96]{2,1,0:T(8,128)(2,1)} %bitcast.97), calls=%async_computation.3 | async-start | bytes 524288 | tf_op jit(solution)/shard_map/all_to_all | solution.py:94
  208.1 2.0 reshape.163
  210.1 2.1 fusion.12
  212.2 7.5 %all-to-all-done.3 = bf16[16,64,96]{2,1,0:T(8,128)(2,1)} async-done(((bf16[16,64,96]{2,1,0:T(8,128)(2,1)}), bf16[16,64,96]{2,1,0:T(8,128)(2,1)}, u32[]{:S(2)}, u32[]{:S(2)}) %all-to-all-start.3) | async-done | bytes 196640 | tf_op jit(solution)/shard_map/all_to_all | solution.py:94
  220.8 1.6 fusion.30
  223.4 1.8 copy.42
  225.2 7.9 %all-to-all-start.4 = ((bf16[16,64,96]{2,1,0:T(8,128)(2,1)}), bf16[16,64,96]{2,1,0:T(8,128)(2,1)}, u32[]{:S(2)}, u32[]{:S(2)}) async-start(bf16[16,64,96]{2,1,0:T(8,128)(2,1)} %bitcast.98), calls=%async_computation.4 | async-start | bytes 524288 | tf_op jit(solution)/shard_map/all_to_all | solution.py:103
  234.9 3.9 %collective-permute-start.6 = (bf16[32,1024]{1,0:T(8,128)(2,1)S(1)}, bf16[32,1024]{1,0:T(8,128)(2,1)S(1)}, u32[]{:S(2)}, u32[]{:S(2)}) collective-permute-start(bf16[32,1024]{1,0:T(8,128)(2,1)S(1)} %slice.78), channel_id=1, source_target_pairs={{0,16},{16,0},{1,17},{17,1},{2,18},{18,2},{3,19},{19,3},{4,20},{20... | collective-permute-start | bytes 196616 | tf_op jit(solution)/shard_map/ppermute | solution.py:116
  238.7 3.4 %all-to-all-done.4 = bf16[16,64,96]{2,1,0:T(8,128)(2,1)} async-done(((bf16[16,64,96]{2,1,0:T(8,128)(2,1)}), bf16[16,64,96]{2,1,0:T(8,128)(2,1)}, u32[]{:S(2)}, u32[]{:S(2)}) %all-to-all-start.4) | async-done | bytes 196640 | tf_op jit(solution)/shard_map/all_to_all | solution.py:103
  243.9 5.4 %all-to-all-start.5 = ((bf16[16,64,96]{2,1,0:T(8,128)(2,1)}), bf16[16,64,96]{2,1,0:T(8,128)(2,1)S(1)}, u32[]{:S(2)}, u32[]{:S(2)}) async-start(bf16[16,64,96]{2,1,0:T(8,128)(2,1)} %broadcast_in_dim.5), calls=%async_computation.5 | async-start | bytes 524288 | tf_op jit(solution)/shard_map/all_to_all | solution.py:105
  250.4 7.8 %all-to-all-done.5 = bf16[16,64,96]{2,1,0:T(8,128)(2,1)S(1)} async-done(((bf16[16,64,96]{2,1,0:T(8,128)(2,1)}), bf16[16,64,96]{2,1,0:T(8,128)(2,1)S(1)}, u32[]{:S(2)}, u32[]{:S(2)}) %all-to-all-start.5) | async-done | bytes 196640 | tf_op jit(solution)/shard_map/all_to_all | solution.py:105
  258.1 5.6 %collective-permute-start.7 = (bf16[1024,96]{1,0:T(8,128)(2,1)S(1)}, bf16[1024,96]{1,0:T(8,128)(2,1)S(1)}, u32[]{:S(2)}, u32[]{:S(2)}) collective-permute-start(bf16[1024,96]{1,0:T(8,128)(2,1)S(1)} %bitcast.99), channel_id=1, source_target_pairs={{0,16},{16,0},{1,17},{17,1},{2,18},{18,2},{3,19},{19,3},{4,20},{20... | collective-permute-start | bytes 589832 | tf_op jit(solution)/shard_map/ppermute | solution.py:108
  263.7 1.6 fusion.17
  (79 shorter events, 27.1 us)
Async XLA Ops:
  7.2 66.9 %copy-start = (bf16[1024,192]{0,1:T(8,128)(2,1)S(1)}, bf16[1024,192]{0,1:T(8,128)(2,1)}, u32[]{:S(2)}) copy-start(bf16[1024,192]{0,1:T(8,128)(2,1)} %param.11) | copy-start | bytes 1179652
  7.2 50.3 %all-gather.3.cloned.1.call-start = ((), (), s32[]{:S(2)}) async-start(), calls=%async_computation.6 | async-start | bytes 2654208 | tf_op jit(solution)/shard_map/all_gather | solution.py:30
  7.9 52.8 %copy-start.14 = (bf16[512,1536]{1,0:T(8,128)(2,1)S(1)}, bf16[512,1536]{1,0:T(8,128)(2,1)}, u32[]{:S(2)}) copy-start(bf16[512,1536]{1,0:T(8,128)(2,1)} %param.6) | copy-start | bytes 4718596
  7.9 33.7 %collective-permute-start.2 = (bf16[512,1536]{1,0:T(8,128)(2,1)}, bf16[512,1536]{1,0:T(8,128)(2,1)S(1)}, u32[]{:S(2)}, u32[]{:S(2)}) collective-permute-start(bf16[512,1536]{1,0:T(8,128)(2,1)} %param.6), channel_id=1, source_target_pairs={{0,32},{32,0},{1,33},{33,1},{2,34},{34,2},{3,35},{35,3},{4,36},{36... | collective-permute-start | bytes 4718600 | tf_op jit(solution)/shard_map/ppermute | solution.py:32
  41.6 20.6 %collective-permute-start.3 = (bf16[512,1536]{1,0:T(8,128)(2,1)S(1)}, bf16[512,1536]{1,0:T(8,128)(2,1)}, u32[]{:S(2)}, u32[]{:S(2)}) collective-permute-start(bf16[512,1536]{1,0:T(8,128)(2,1)S(1)} %collective-permute-done.2), channel_id=1, source_target_pairs={{0,16},{16,0},{1,17},{17,1},{2,18},{18,2},{3,19},{19,3},{4,20},{20... | collective-permute-start | bytes 4718600 | tf_op jit(solution)/shard_map/ppermute | solution.py:34
  49.5 15.5 %collective-permute-start.1 = (bf16[512,1536]{1,0:T(8,128)(2,1)}, bf16[512,1536]{1,0:T(8,128)(2,1)}, u32[]{:S(2)}, u32[]{:S(2)}) collective-permute-start(bf16[512,1536]{1,0:T(8,128)(2,1)} %param.6), channel_id=1, source_target_pairs={{0,16},{16,0},{1,17},{17,1},{2,18},{18,2},{3,19},{19,3},{4,20},{20... | collective-permute-start | bytes 4718600 | tf_op jit(solution)/shard_map/ppermute | solution.py:33
  57.5 3.2 %copy-start.13 = (bf16[768,1536]{1,0:T(8,128)(2,1)S(1)}, bf16[768,1536]{1,0:T(8,128)(2,1)}, u32[]{:S(2)}) copy-start(bf16[768,1536]{1,0:T(8,128)(2,1)} %all-gather.3.cloned.1.call-done) | copy-start | bytes 7077892
  70.1 37.4 %all-to-all-start.1 = ((bf16[4,2,4,2,32,768]{5,4,2,3,1,0:T(8,128)(2,1)}), bf16[4,2,4,2,32,768]{5,4,2,3,1,0:T(8,128)(2,1)S(1)}, u32[]{:S(2)}, u32[]{:S(2)}) async-start(bf16[4,2,4,2,32,768]{5,4,2,3,1,0:T(8,128)(2,1)} %maximum_bitcast_fusion), calls=%async_computation.1 | async-start | bytes 6291456 | tf_op jit(solution)/shard_map/all_to_all | solution.py:73
  110.7 37.2 %all-to-all-start = ((bf16[4,4,96,1024]{3,2,1,0:T(8,128)(2,1)}), bf16[4,4,96,1024]{3,2,1,0:T(8,128)(2,1)}, u32[]{:S(2)}, u32[]{:S(2)}) async-start(bf16[4,4,96,1024]{3,2,1,0:T(8,128)(2,1)} %broadcast_in_dim.4), calls=%async_computation | async-start | bytes 6291456 | tf_op jit(solution)/shard_map/all_to_all | solution.py:51
  115.3 17.6 %collective-permute-start = (bf16[512,1024]{1,0:T(8,128)(2,1)}, bf16[512,1024]{1,0:T(8,128)(2,1)}, u32[]{:S(2)}, u32[]{:S(2)}) collective-permute-start(bf16[512,1024]{1,0:T(8,128)(2,1)} %param.9), channel_id=1, source_target_pairs={{0,16},{16,0},{1,17},{17,1},{2,18},{18,2},{3,19},{19,3},{4,20},{20... | collective-permute-start | bytes 3145736 | tf_op jit(solution)/shard_map/ppermute | solution.py:36
  124.2 4.3 %copy-start.1 = (bf16[512,1024]{1,0:T(8,128)(2,1)S(1)}, bf16[512,1024]{1,0:T(8,128)(2,1)}, u32[]{:S(2)}) copy-start(bf16[512,1024]{1,0:T(8,128)(2,1)} %param.9) | copy-start | bytes 3145732
  126.6 3.6 %collective-permute-start.4 = (bf16[32,8,2,96]{3,1,0,2:T(8,128)(2,1)}, bf16[32,8,2,96]{3,1,0,2:T(8,128)(2,1)}, u32[]{:S(2)}, u32[]{:S(2)}) collective-permute-start(bf16[32,8,2,96]{3,1,0,2:T(8,128)(2,1)} %bitcast.85), channel_id=1, source_target_pairs={{0,16},{16,0},{1,17},{17,1},{2,18},{18,2},{3,19},{19,3},{4,20},{20... | collective-permute-start | bytes 294920 | tf_op jit(solution)/shard_map/ppermute | solution.py:60
  131.2 0.8 copy-start.3
  137.7 16.6 %copy-start.2 = (bf16[512,1024]{1,0:T(8,128)(2,1)S(1)}, bf16[512,1024]{1,0:T(8,128)(2,1)}, u32[]{:S(2)}) copy-start(bf16[512,1024]{1,0:T(8,128)(2,1)} %param.9) | copy-start | bytes 3145732
  137.7 16.6 %copy-start.12 = (f32[1024]{0:T(1024)S(1)}, f32[1024]{0:T(1024)}, u32[]{:S(2)}) copy-start(f32[1024]{0:T(1024)} %param.10) | copy-start | bytes 12292
  147.9 24.0 %all-to-all-start.2 = ((bf16[8,64,768]{2,1,0:T(8,128)(2,1)}), bf16[8,64,768]{2,1,0:T(8,128)(2,1)}, u32[]{:S(2)}, u32[]{:S(2)}) async-start(bf16[8,64,768]{2,1,0:T(8,128)(2,1)} %bitcast.18), calls=%async_computation.2 | async-start | bytes 1572864 | tf_op jit(solution)/shard_map/all_to_all | solution.py:77
  156.5 1.0 copy-start.4
  156.5 1.3 copy-start.6
  157.8 2.6 copy-start.8
  157.8 2.6 copy-start.10
  175.9 12.8 %copy-start.9 = (bf16[32,1024]{1,0:T(8,128)(2,1)S(1)}, bf16[32,1024]{1,0:T(8,128)(2,1)}, u32[]{:S(2)}) copy-start(bf16[32,1024]{1,0:T(8,128)(2,1)} %copy-done.8) | copy-start | bytes 196612
  175.9 12.8 %copy-start.11 = (bf16[32,1024]{1,0:T(8,128)(2,1)S(1)}, bf16[32,1024]{1,0:T(8,128)(2,1)}, u32[]{:S(2)}) copy-start(bf16[32,1024]{1,0:T(8,128)(2,1)} %copy-done.10) | copy-start | bytes 196612
  179.9 20.2 %collective-permute-start.5 = (f32[2,2,32]{2,1,0:T(2,128)}, f32[2,2,32]{2,1,0:T(2,128)S(1)}, u32[]{:S(2)}, u32[]{:S(2)}) collective-permute-start(f32[2,2,32]{2,1,0:T(2,128)} %pad_maximum_fusion.5), channel_id=1, source_target_pairs={{0,16},{16,0},{1,17},{17,1},{2,18},{18,2},{3,19},{19,3},{4,20},{20... | collective-permute-start | bytes 1544 | tf_op jit(solution)/shard_map/ppermute | solution.py:85
  203.9 15.8 %all-to-all-start.3 = ((bf16[16,64,96]{2,1,0:T(8,128)(2,1)}), bf16[16,64,96]{2,1,0:T(8,128)(2,1)}, u32[]{:S(2)}, u32[]{:S(2)}) async-start(bf16[16,64,96]{2,1,0:T(8,128)(2,1)} %bitcast.97), calls=%async_computation.3 | async-start | bytes 524288 | tf_op jit(solution)/shard_map/all_to_all | solution.py:94
  219.7 2.7 copy-start.5
  225.2 17.0 %all-to-all-start.4 = ((bf16[16,64,96]{2,1,0:T(8,128)(2,1)}), bf16[16,64,96]{2,1,0:T(8,128)(2,1)}, u32[]{:S(2)}, u32[]{:S(2)}) async-start(bf16[16,64,96]{2,1,0:T(8,128)(2,1)} %bitcast.98), calls=%async_computation.4 | async-start | bytes 524288 | tf_op jit(solution)/shard_map/all_to_all | solution.py:103
  233.1 1.4 copy-start.7
  234.9 14.5 %collective-permute-start.6 = (bf16[32,1024]{1,0:T(8,128)(2,1)S(1)}, bf16[32,1024]{1,0:T(8,128)(2,1)S(1)}, u32[]{:S(2)}, u32[]{:S(2)}) collective-permute-start(bf16[32,1024]{1,0:T(8,128)(2,1)S(1)} %slice.78), channel_id=1, source_target_pairs={{0,16},{16,0},{1,17},{17,1},{2,18},{18,2},{3,19},{19,3},{4,20},{20... | collective-permute-start | bytes 196616 | tf_op jit(solution)/shard_map/ppermute | solution.py:116
  243.9 14.2 %all-to-all-start.5 = ((bf16[16,64,96]{2,1,0:T(8,128)(2,1)}), bf16[16,64,96]{2,1,0:T(8,128)(2,1)S(1)}, u32[]{:S(2)}, u32[]{:S(2)}) async-start(bf16[16,64,96]{2,1,0:T(8,128)(2,1)} %broadcast_in_dim.5), calls=%async_computation.5 | async-start | bytes 524288 | tf_op jit(solution)/shard_map/all_to_all | solution.py:105
  258.1 7.2 %collective-permute-start.7 = (bf16[1024,96]{1,0:T(8,128)(2,1)S(1)}, bf16[1024,96]{1,0:T(8,128)(2,1)S(1)}, u32[]{:S(2)}, u32[]{:S(2)}) collective-permute-start(bf16[1024,96]{1,0:T(8,128)(2,1)S(1)} %bitcast.99), channel_id=1, source_target_pairs={{0,16},{16,0},{1,17},{17,1},{2,18},{18,2},{3,19},{19,3},{4,20},{20... | collective-permute-start | bytes 589832 | tf_op jit(solution)/shard_map/ppermute | solution.py:108
Sparse Core Ops, SparseCore 0:
  10.1 47.3 all-gather.2

commit v2 on v0

v2 whole, which is shorter than its diff:
```python
import functools

import jax
import jax.numpy as jnp
from jax import lax
from jax.experimental import pallas as pl
from jax.experimental.pallas import tpu as pltpu
from jax.sharding import Mesh, PartitionSpec as P

AXES = ("z", "yl", "c", "yh", "x")
SIZES = (8, 2, 2, 4, 4)
NZ, NYH, NX = 8, 4, 4
NT = NYH * NX
TENSOR = ("yh", "x")
REPLICA = ("z", "yl")
SWAP = [(0, 1), (1, 0)]
F32 = jnp.float32
BF16 = jnp.bfloat16
VMEM = pl.BlockSpec(memory_space=pltpu.VMEM)
SMEM = pl.BlockSpec(memory_space=pltpu.SMEM)
ANY = pl.BlockSpec(memory_space=pl.ANY)
PARAMS = pltpu.CompilerParams(vmem_limit_bytes=16 * 1024 * 1024)


def dot_nt(a, b):
    return lax.dot_general(a, b, (((1,), (1,)), ((), ())), preferred_element_type=F32)


def product_kernel(owners, own, core, other, both, w, mine, rest):
    depth = own.shape[-1]
    own_rows = own.shape[2]
    lhs = jnp.concatenate(
        [ref[...].reshape(NYH * own_rows, depth) for ref in (own, core, other, both)], axis=0
    )
    width = NYH * w.shape[2]
    rhs = w[...].reshape(width, depth)
    part = dot_nt(lhs, rhs).astype(BF16).reshape(2, 2, NYH, own_rows, width)
    for c in range(2):
        mine[0, :, c] = part[0, c]
        rest[0, :, c] = part[1, c]


def product(owners, blocks, w):
    count = owners.shape[0]
    rows, depth = blocks[0].shape
    own_rows = rows // NT
    half = w.shape[0] // NZ
    width = NYH * half
    block = pl.BlockSpec((NYH, 1, own_rows, depth), lambda i, j, o: (0, o[i], 0, 0))
    out = pl.BlockSpec((1, NYH, 2, own_rows, width), lambda i, j, o: (i, 0, 0, 0, j))
    shape = jax.ShapeDtypeStruct((count, NYH, 2, own_rows, 2 * width), BF16)
    return pl.pallas_call(
        product_kernel,
        grid_spec=pltpu.PrefetchScalarGridSpec(
            num_scalar_prefetch=1,
            grid=(count, 2),
            in_specs=[block] * 4
            + [pl.BlockSpec((NYH, 1, half, depth), lambda i, j, o: (0, j, 0, 0))],
            out_specs=[out, out],
        ),
        out_shape=[shape, shape],
        compiler_params=pltpu.CompilerParams(vmem_limit_bytes=56 * 1024 * 1024),
        cost_estimate=pl.CostEstimate(
            flops=2 * count * rows * 2 * width * depth,
            bytes_accessed=count * 5_000_000,
            transcendentals=0,
        ),
        name="product",
    )(
        owners,
        *[b.reshape(NYH, NX, own_rows, depth) for b in blocks],
        w.reshape(NYH, 2, half, depth),
    )


def relay_kernel(mine, rest, from_low, from_high, up, down):
    up[0] = (mine[0].astype(F32) + from_low[0].astype(F32)).astype(BF16)
    up[1] = rest[0]
    down[0] = mine[1]
    down[1] = (rest[1].astype(F32) + from_high[0].astype(F32)).astype(BF16)


def relay(mine, rest, from_low, from_high):
    _, _, _, own_rows, cols = mine.shape
    pair = pl.BlockSpec((2, 1, 2, own_rows, cols), lambda i: (0, i, 0, 0, 0))
    single = pl.BlockSpec((1, 1, 2, own_rows, cols), lambda i: (0, i, 0, 0, 0))
    shape = jax.ShapeDtypeStruct((2, NYH, 2, own_rows, cols), BF16)
    return pl.pallas_call(
        relay_kernel,
        grid=(NYH,),
        in_specs=[pair, pair, single, single],
        out_specs=[pair, pair],
        out_shape=[shape, shape],
        compiler_params=PARAMS,
        name="relay",
    )(mine, rest, from_low, from_high)


def sum_x_kernel(yl, mine, rest, low, high, out):
    for step, ref in enumerate((mine, rest)):
        total = ref[0].astype(F32) + low[step].astype(F32) + high[step].astype(F32)
        out[:, (yl[0] + step) % 2] = total.astype(BF16)


def sum_x(yl, mine, rest, low, high):
    _, _, _, own_rows, cols = mine.shape
    single = pl.BlockSpec((1, 1, 2, own_rows, cols), lambda i: (2, i, 0, 0, 0))
    pair = pl.BlockSpec((2, 1, 2, own_rows, cols), lambda i: (0, i, 0, 0, 0))
    return pl.pallas_call(
        sum_x_kernel,
        grid=(NYH,),
        in_specs=[SMEM, single, single, pair, pair],
        out_specs=pl.BlockSpec((1, 2, 2, own_rows, cols), lambda i: (i, 0, 0, 0, 0)),
        out_shape=jax.ShapeDtypeStruct((NYH, 2, 2, own_rows, cols), BF16),
        compiler_params=PARAMS,
        name="sum_x",
    )(yl, mine, rest, low, high)


def features_kernel(got, resid, feats, stats):
    half = resid.shape[1] // NT
    for x in range(NX):
        xh, xl = divmod(x, 2)
        lanes = slice(xh * NYH * half, (xh + 1) * NYH * half)
        total = got[0, xl, :, lanes].astype(F32)
        for src in range(1, NYH):
            total = total + got[src, xl, :, lanes].astype(F32)
        for yh in range(NYH):
            place = slice((yh * NX + x) * half, (yh * NX + x + 1) * half)
            feats[:, place] = total[:, yh * half : (yh + 1) * half] + resid[:, place].astype(F32)
    whole = feats[...]
    mean = jnp.mean(whole, axis=1, keepdims=True)
    square = jnp.sum((whole - mean) ** 2, axis=1, keepdims=True)
    stats[0] = jnp.broadcast_to(mean, stats.shape[1:])
    stats[1] = jnp.broadcast_to(square, stats.shape[1:])


def features(got, resid):
    rows, cols = resid.shape
    return pl.pallas_call(
        features_kernel,
        in_specs=[VMEM, VMEM],
        out_specs=[VMEM, VMEM],
        out_shape=[
            jax.ShapeDtypeStruct((rows, cols), F32),
            jax.ShapeDtypeStruct((2, rows, 128), F32),
        ],
        compiler_params=PARAMS,
        name="features",
    )(got, resid)


def delta_kernel(feats, mine, other, pred, delta, send):
    rows, count = feats.shape
    own = rows // 2
    mean_a, square_a = mine[0, :, :1], mine[1, :, :1]
    mean_b = jnp.concatenate([other[0, own:, :1], other[0, :own, :1]], axis=0)
    square_b = jnp.concatenate([other[1, own:, :1], other[1, :own, :1]], axis=0)
    gap = mean_a - mean_b
    mean = 0.5 * (mean_a + mean_b)
    variance = (square_a + square_b + gap * gap * (0.5 * count)) / (2 * count)
    scale = lax.rsqrt(variance + 1e-06)
    target = ((feats[...] - mean) * scale).astype(BF16)
    result = (pred[...] - target.astype(F32)).astype(BF16)
    delta[...] = result
    half = count // NT
    for t in range(NT):
        send[t] = result[:, t * half : (t + 1) * half]


def deltas(feats, mine, other, pred):
    rows, count = feats.shape
    return pl.pallas_call(
        delta_kernel,
        in_specs=[VMEM] * 4,
        out_specs=[VMEM] * 2,
        out_shape=[
            jax.ShapeDtypeStruct((rows, count), BF16),
            jax.ShapeDtypeStruct((NT, rows, count // NT), BF16),
        ],
        compiler_params=PARAMS,
        name="delta",
    )(feats, mine, other, pred)


def resid_kernel(core, resid, keep, send):
    half = resid.shape[1] // (2 * NT)
    for t in range(NT):
        start = 2 * half * t
        place = slice(t * half, (t + 1) * half)
        first = resid[:, start : start + half]
        second = resid[:, start + half : start + 2 * half]
        keep[:, place] = jnp.where(core[0] == 0, first, second)
        send[:, place] = jnp.where(core[0] == 0, second, first)


def resid_halves(resid, core):
    rows, cols = resid.shape
    shape = jax.ShapeDtypeStruct((rows, cols // 2), BF16)
    return pl.pallas_call(
        resid_kernel,
        in_specs=[SMEM, VMEM],
        out_specs=[VMEM] * 2,
        out_shape=[shape, shape],
        compiler_params=PARAMS,
        name="resid_halves",
    )(core, resid)


def norm_kernel(mine, inputs, other, gain, normed, owned):
    scale = gain[...]

    def norm(block):
        values = block.astype(F32)
        rms = jnp.sqrt(jnp.mean(values * values, axis=-1, keepdims=True) + 1e-06)
        return (values / rms * scale).astype(BF16)

    for c, ref in enumerate((inputs, other)):
        for t in range(NT):
            normed[t, c] = norm(ref[t])
    owned[...] = normed[mine[0]]


def norms(mine, inputs, other, gain):
    rows, width = inputs.shape
    own = rows // NT
    return pl.pallas_call(
        norm_kernel,
        in_specs=[SMEM] + [VMEM] * 3,
        out_specs=[VMEM] * 2,
        out_shape=[
            jax.ShapeDtypeStruct((NT, 2, own, width), BF16),
            jax.ShapeDtypeStruct((2, own, width), BF16),
        ],
        compiler_params=PARAMS,
        name="norms",
    )(mine, inputs.reshape(NT, own, width), other.reshape(NT, own, width), gain.reshape(1, width))


def grad_kernel(delta, normed, out, rows, sems):
    parts = sems.shape[0]
    size = rows.shape[0] // parts
    copies = [
        pltpu.make_async_copy(
            normed.at[pl.ds(i * size, size)], rows.at[pl.ds(i * size, size)], sems.at[i]
        )
        for i in range(parts)
    ]
    for copy in copies:
        copy.start()
    for copy in copies:
        copy.wait()
    part = lax.dot_general(
        delta[...], rows[...], (((0,), (0,)), ((), ())), preferred_element_type=F32
    ).astype(BF16)
    _, high, wide = out.shape
    across = part.shape[1] // wide
    for i in range(out.shape[0]):
        a, b = divmod(i, across)
        out[i] = part[a * high : (a + 1) * high, b * wide : (b + 1) * wide]


def grad_part(delta, normed):
    shape = (2 * NZ, delta.shape[1] // 2, normed.shape[1] // NZ)
    return pl.pallas_call(
        grad_kernel,
        in_specs=[VMEM, ANY],
        out_specs=VMEM,
        out_shape=jax.ShapeDtypeStruct(shape, BF16),
        scratch_shapes=[pltpu.VMEM(normed.shape, BF16), pltpu.SemaphoreType.DMA((8,))],
        compiler_params=PARAMS,
        name="grad_part",
    )(delta, normed)


def sum_grad_kernel(got, out):
    total = got[0].astype(F32)
    for i in range(1, got.shape[0]):
        total = total + got[i].astype(F32)
    out[...] = jnp.broadcast_to(total.astype(BF16)[None], out.shape)


def sum_grad(got):
    return pl.pallas_call(
        sum_grad_kernel,
        in_specs=[VMEM],
        out_specs=VMEM,
        out_shape=jax.ShapeDtypeStruct(got.shape, BF16),
        compiler_params=PARAMS,
        name="sum_grad",
    )(got)


def join_kernel(divisor, core, mine, other, out):
    pieces, high, wide = mine.shape
    half = out.shape[0] // 2
    across = out.shape[1] // wide
    for ref, start in ((mine, core[0] * half), (other, (1 - core[0]) * half)):
        for i in range(pieces):
            a, b = divmod(i, across)
            rows = pl.ds(pl.multiple_of(start + a * high, 16), high)
            out[rows, b * wide : (b + 1) * wide] = ref[i].astype(F32) / divisor


def join(mine, other, core, divisor):
    pieces, high, wide = mine.shape
    return pl.pallas_call(
        functools.partial(join_kernel, divisor),
        in_specs=[SMEM, VMEM, VMEM],
        out_specs=VMEM,
        out_shape=jax.ShapeDtypeStruct((4 * high, pieces * wide // 2), F32),
        compiler_params=PARAMS,
        name="join",
    )(core, mine, other)


def send_x(block, step):
    return lax.ppermute(block, "x", [(i, (i + step) % NX) for i in range(NX)])


def local(hidden, resid, down_w, inputs, gain, head):
    rows, depth = hidden.shape
    half = down_w.shape[1]
    width = inputs.shape[1]
    own = rows // NT
    cols = NZ * half
    yl = lax.axis_index("yl").astype(jnp.int32).reshape(1)
    core_id = lax.axis_index("c").astype(jnp.int32)
    core = core_id.reshape(1)
    mine = lax.axis_index(TENSOR)

    w = lax.all_gather(down_w.T, "z", axis=0, tiled=True)

    hidden_y = lax.ppermute(hidden, "yl", SWAP)
    hidden_c = lax.ppermute(hidden, "c", SWAP)
    inputs_c = lax.ppermute(inputs, "c", SWAP)
    head_half = lax.dynamic_slice_in_dim(head.T, core_id * half, half, 0)
    head_x = lax.all_to_all(
        jnp.broadcast_to(head_half[None], (NX, half, width)), "x", 0, 0, tiled=True
    )
    resid_keep, resid_send = resid_halves(resid, core)
    resid_own = jnp.concatenate([resid_keep, lax.ppermute(resid_send, "c", SWAP)], axis=0)
    normed, normed_own = norms(mine.astype(jnp.int32).reshape(1), inputs, inputs_c, gain)
    hidden_y, hidden_c, head_x, resid_own, normed, normed_own = lax.optimization_barrier(
        (hidden_y, hidden_c, head_x, resid_own, normed, normed_own)
    )
    hidden_yc = lax.ppermute(hidden_y, "c", SWAP)
    w, head_x = lax.optimization_barrier((w, head_x))
    head_all = lax.all_gather(head_x, "yh", axis=0).reshape(2 * cols, width)

    x = lax.axis_index("x").astype(jnp.int32)
    blocks = (hidden, hidden_c, hidden_y, hidden_yc)
    far_mine, far_rest = product(jnp.stack([(x + 2) % NX]), blocks, w)
    from_low = send_x(far_mine, 1)
    from_high = send_x(far_rest, -1)
    mine_parts, rest_parts = product(jnp.stack([(x + 1) % NX, (x + 3) % NX, x]), blocks, w)
    up, down = relay(mine_parts, rest_parts, from_low, from_high)
    low, high = send_x(up, 1), send_x(down, -1)

    send_y = sum_x(yl, mine_parts, rest_parts, low, high).reshape(2 * NYH, 2 * own, cols)
    got_y = lax.all_to_all(send_y, ("yh", "yl"), 0, 0, tiled=True)
    pred = dot_nt(normed_own.reshape(2 * own, width), head_all)
    feats, stats = features(got_y.reshape(NYH, 2, 2 * own, cols), resid_own)

    delta, send_t = deltas(feats, stats, lax.ppermute(stats, "c", SWAP), pred)

    got_t = lax.all_to_all(send_t, TENSOR, 0, 0, tiled=True)
    head_part = grad_part(got_t.reshape(2 * rows, half), normed.reshape(2 * rows, width))
    got_g = lax.all_to_all(head_part, REPLICA, 0, 0, tiled=True)
    all_g = lax.all_to_all(sum_grad(got_g), REPLICA, 0, 0, tiled=True)
    head_grad = join(all_g, lax.ppermute(all_g, "c", SWAP), core, float(rows)).T

    dn = jnp.dot(delta, head_all, preferred_element_type=F32)
    dnormed = dn[:own] + lax.ppermute(dn[own:].astype(BF16), "c", SWAP).astype(F32)
    values = lax.dynamic_slice_in_dim(inputs, mine * own, own, 0).astype(F32)
    rms = jnp.sqrt(jnp.mean(values * values, axis=1, keepdims=True) + 1e-06)
    scaled = gain * dnormed
    total = jnp.sum(scaled * values, axis=1, keepdims=True)
    input_grad = scaled / rms - values * total / (width * rms * rms * rms)
    return input_grad.astype(BF16), head_grad


def solution(mesh):
    fine = Mesh(mesh.devices.reshape(SIZES), AXES)
    dp, tensor = ("z", "yl", "c"), ("yh", "x")
    in_specs = (P(dp, tensor), P(dp + tensor, None), P(tensor, dp), P(dp, None), P(), P(None, tensor))
    out_specs = (P(dp + tensor, None), P(None, tensor))
    return jax.shard_map(local, mesh=fine, in_specs=in_specs, out_specs=out_specs, check_vma=False)
```

time: 601 us -> 222 us (0.37)
  waiting for transfers between devices: 558 us -> 55.1 us
  starting transfers between devices: 0.2 us -> 61.7 us
  blocking collectives: 0 us -> 47.3 us
  Pallas kernels: 0 us -> 25.6 us
  matrix products: 14.5 us -> 5.68 us
  other arithmetic: 12 us -> 3.94 us
    psum x1 -> x0, waiting for transfers between devices: 213 us -> none  [local(): lax.psum(local_grad.astype(jnp.bfloat16), 'dp').astype(jnp.float32)]
    reduce_scatter x2 -> x0, waiting for transfers between devices: 188 us -> none  [the longest x1 94.7 us: local(): lax.psum_scatter(lax.dot_general(delta, head, (((1,), (1,)), ((), ())), p...]
    all_gather x2, waiting for transfers between devices: 156 us -> 16.1 us  [the longest x1 16 us: local(): w = lax.all_gather(down_w.T, 'z', axis=0, tiled=True)]
    all_to_all x0 -> x2, blocking collectives: none -> 47.3 us  [the longest x1 31.4 us: local(): got_y = lax.all_to_all(send_y, ('yh', 'yl'), 0, 0, tiled=True)]
    ppermute x0 -> x12, starting transfers between devices: none -> 43.8 us  [the longest x4 13 us: send_x(): return lax.ppermute(block, 'x', [(i, (i + step) % NX) for i in range(NX)])]
    pallas_call x0 -> x11, Pallas kernels: none -> 25.6 us  [the longest x2 15.4 us: product(): pl.pallas_call(product_kernel, grid_spec=pltpu.PrefetchScalarGridSpec(num...]
    ppermute x0 -> x12, waiting for transfers between devices: none -> 23.8 us  [the longest x4 15.9 us: send_x(): return lax.ppermute(block, 'x', [(i, (i + step) % NX) for i in range(NX)])]
    all_to_all x0 -> x3, starting transfers between devices: none -> 17.8 us  [the longest x1 8.9 us: local(): got_g = lax.all_to_all(head_part, REPLICA, 0, 0, tiled=True)]
  transfers between devices with their start and end apart: 5 -> 17, of which waited for: 5 -> 9; matrix products, arithmetic and copies ran while one was open for 1% -> 5% of each run, Pallas kernels for 0% -> 10%
where the time goes in v2:
time: 222 us; the launch traced here: 220 us
  starting transfers between devices  61.7 us (28%)
  waiting for transfers between devices  55.1 us (25%)
  blocking collectives  47.3 us (21%)
  Pallas kernels  25.6 us (12%)
  between operations  14.4 us (6%)
  local copies, waits for them, and re-layouts  6.76 us (3%)
  matrix products  5.68 us (3%)
  other arithmetic  3.94 us (2%)
    all_to_all x1, blocking collectives, local(): got_y = lax.all_to_all(send_y, ('yh', 'yl'), 0, 0, tiled=True)  31.4 us
    all_gather x1, waiting for transfers between devices, local(): w = lax.all_gather(down_w.T, 'z', axis=0, tiled=True)  16 us
    ppermute x4, waiting for transfers between devices, send_x(): return lax.ppermute(block, 'x', [(i, (i + step) % NX) for i in range(NX)])  15.9 us
    all_to_all x1, blocking collectives, local(): got_t = lax.all_to_all(send_t, TENSOR, 0, 0, tiled=True)  15.9 us
    pallas_call x2, Pallas kernels, product(): pl.pallas_call(product_kernel, grid_spec=pltpu.PrefetchScalarGridSpec(num...  15.4 us
    ppermute x4, starting transfers between devices, send_x(): return lax.ppermute(block, 'x', [(i, (i + step) % NX) for i in range(NX)])  13 us
    all_to_all x1, starting transfers between devices, local(): got_g = lax.all_to_all(head_part, REPLICA, 0, 0, tiled=True)  8.9 us
    all_to_all x1, waiting for transfers between devices, local(): all_g = lax.all_to_all(sum_grad(got_g), REPLICA, 0, 0, tiled=True)  7.58 us
  transfers between devices with their start and end apart: 17, of which 9 were waited for; matrix products, arithmetic and copies ran while one was open for 5% of the time, Pallas kernels for 10%

profile of v2, /device:TPU:1, one launch (start us, length us, event | category | flops | bytes accessed | tf_op | source)
XLA Modules:
  0.0 220.4 jit_solution(13862147878328042193)
XLA Ops:
  7.3 0.7 all-gather.4.cloned.1.call-update
  7.9 4.0 %collective-permute-start = (bf16[512,1536]{1,0:T(8,128)(2,1)}, bf16[512,1536]{1,0:T(8,128)(2,1)}, u32[]{:S(2)}, u32[]{:S(2)}) collective-permute-start(bf16[512,1536]{1,0:T(8,128)(2,1)} %param.6), channel_id=1, source_target_pairs={{0,32},{32,0},{1,33},{33,1},{2,34},{34,2},{3,35},{35,3},{4,36},{36... | collective-permute-start | bytes 4718600 | tf_op jit(solution)/shard_map/ppermute | solution.py:334
  12.0 6.7 %collective-permute-start.1 = (bf16[512,1536]{1,0:T(8,128)(2,1)}, bf16[512,1536]{1,0:T(8,128)(2,1)}, u32[]{:S(2)}, u32[]{:S(2)}) collective-permute-start(bf16[512,1536]{1,0:T(8,128)(2,1)} %param.6), channel_id=1, source_target_pairs={{0,16},{16,0},{1,17},{17,1},{2,18},{18,2},{3,19},{19,3},{4,20},{20... | collective-permute-start | bytes 4718600 | tf_op jit(solution)/shard_map/ppermute | solution.py:335
  18.7 1.9 collective-permute-start.3
  20.7 1.0 broadcast_in_dim.4
  21.6 4.2 %all-to-all-start = ((bf16[4,96,1024]{2,1,0:T(8,128)(2,1)}), bf16[4,96,1024]{2,1,0:T(8,128)(2,1)}, u32[]{:S(2)}, u32[]{:S(2)}) async-start(bf16[4,96,1024]{2,1,0:T(8,128)(2,1)} %broadcast_in_dim.4), calls=%async_computation | async-start | bytes 1572864 | tf_op jit(solution)/shard_map/all_to_all | solution.py:338
  25.9 1.1 resid_halves.1
  26.9 2.4 %collective-permute-start.2 = (bf16[32,1536]{1,0:T(8,128)(2,1)S(1)}, bf16[32,1536]{1,0:T(8,128)(2,1)S(1)}, u32[]{:S(2)}, u32[]{:S(2)}) collective-permute-start(bf16[32,1536]{1,0:T(8,128)(2,1)S(1)} %get-tuple-element.25), channel_id=1, source_target_pairs={{0,16},{16,0},{1,17},{17,1},{2,18},{18,2},{3,19},{19,3},{4,20},{20... | collective-permute-start | bytes 294920 | tf_op jit(solution)/shard_map/ppermute | solution.py:342
  29.4 0.9 collective-permute-done.2
  30.3 0.7 pad_maximum_fusion.resid
  31.0 1.0 norms.1
  32.0 1.3 copy-done.5
  33.9 3.8 %all-to-all-done = bf16[4,96,1024]{2,1,0:T(8,128)(2,1)} async-done(((bf16[4,96,1024]{2,1,0:T(8,128)(2,1)}), bf16[4,96,1024]{2,1,0:T(8,128)(2,1)}, u32[]{:S(2)}, u32[]{:S(2)}) %all-to-all-start) | async-done | bytes 786464 | tf_op jit(solution)/shard_map/all_to_all | solution.py:338
  37.8 3.7 %collective-permute-done = bf16[512,1536]{1,0:T(8,128)(2,1)} collective-permute-done((bf16[512,1536]{1,0:T(8,128)(2,1)}, bf16[512,1536]{1,0:T(8,128)(2,1)}, u32[]{:S(2)}, u32[]{:S(2)}) %collective-permute-start) | collective-permute-done | bytes 1572896 | tf_op jit(solution)/shard_map/ppermute | solution.py:334
  41.5 16.0 %all-gather.4.cloned.1.call-done = bf16[768,1536]{1,0:T(8,128)(2,1)} async-done(((bf16[96,1536]{1,0:T(8,128)(2,1)}), bf16[768,1536]{1,0:T(8,128)(2,1)}) %all-gather.4.cloned.1.call-update) | async-done | bytes 2359312 | tf_op jit(solution)/shard_map/all_gather | solution.py:332
  57.6 5.8 %collective-permute-start.4 = (bf16[512,1536]{1,0:T(8,128)(2,1)}, bf16[512,1536]{1,0:T(8,128)(2,1)S(1)}, u32[]{:S(2)}, u32[]{:S(2)}) collective-permute-start(bf16[512,1536]{1,0:T(8,128)(2,1)} %collective-permute-done), channel_id=1, source_target_pairs={{0,16},{16,0},{1,17},{17,1},{2,18},{18,2},{3,19},{19,3},{4,20},{20... | collective-permute-start | bytes 4718600 | tf_op jit(solution)/shard_map/ppermute | solution.py:347
  63.4 3.2 %collective-permute-done.4 = bf16[512,1536]{1,0:T(8,128)(2,1)S(1)} collective-permute-done((bf16[512,1536]{1,0:T(8,128)(2,1)}, bf16[512,1536]{1,0:T(8,128)(2,1)S(1)}, u32[]{:S(2)}, u32[]{:S(2)}) %collective-permute-start.4) | collective-permute-done | bytes 1572896 | tf_op jit(solution)/shard_map/ppermute | solution.py:347
  66.6 1.2 copy-done.13
  67.8 4.5 %product.3 = (bf16[1,4,2,32,768]{4,3,2,1,0:T(8,128)(2,1)}, bf16[1,4,2,32,768]{4,3,2,1,0:T(8,128)(2,1)}) custom-call(s32[1]{0:T(128)} %bitcast.16.owners, bf16[4,4,32,1536]{3,2,1,0:T(8,128)(2,1)} %bitcast.41, bf16[4,4,32,1536]{3,2,1,0:T(8,128)(2,1)} %bitcast.11.core, bf16[4,4,32,1536]{3,2,1,0:T(8,128)(2,1)} %bitcast.12.other, ...), custom_call_target="tpu_custom_call" | custom-call | flops 1207959552 | bytes 5000000 | tf_op jit(solution)/shard_map/product/pallas_call | solution.py:52
  72.3 3.1 %collective-permute-start.5 = (bf16[1,4,2,32,768]{4,3,2,1,0:T(8,128)(2,1)}, bf16[1,4,2,32,768]{4,3,2,1,0:T(8,128)(2,1)S(1)}, u32[]{:S(2)}, u32[]{:S(2)}) collective-permute-start(bf16[1,4,2,32,768]{4,3,2,1,0:T(8,128)(2,1)} %get-tuple-element.34), channel_id=1, source_target_pairs={{0,1},{1,2},{2,3},{3,0},{4,5},{5,6},{6,7},{7,4},{8,9},{9,10},{10,1... | collective-permute-start | bytes 1179656 | tf_op jit(solution)/shard_map/ppermute | solution.py:318
  75.4 3.4 %collective-permute-start.6 = (bf16[1,4,2,32,768]{4,3,2,1,0:T(8,128)(2,1)}, bf16[1,4,2,32,768]{4,3,2,1,0:T(8,128)(2,1)S(1)}, u32[]{:S(2)}, u32[]{:S(2)}) collective-permute-start(bf16[1,4,2,32,768]{4,3,2,1,0:T(8,128)(2,1)} %get-tuple-element.35), channel_id=1, source_target_pairs={{0,3},{1,0},{2,1},{3,2},{4,7},{5,4},{6,5},{7,6},{8,11},{9,8},{10,9... | collective-permute-start | bytes 1179656 | tf_op jit(solution)/shard_map/ppermute | solution.py:318
  78.8 0.7 pad_add_fusion.owners
  79.4 10.9 %product.2 = (bf16[3,4,2,32,768]{4,3,2,1,0:T(8,128)(2,1)}, bf16[3,4,2,32,768]{4,3,2,1,0:T(8,128)(2,1)}) custom-call(s32[3]{0:T(128)} %pad_add_fusion.owners, bf16[4,4,32,1536]{3,2,1,0:T(8,128)(2,1)} %bitcast.42, bf16[4,4,32,1536]{3,2,1,0:T(8,128)(2,1)} %bitcast.11.core, bf16[4,4,32,1536]{3,2,1,0:T(8,128)(2,1)} %bitcast.12.other, ...), custom_call_target="tpu_custom_call" | custom-call | flops 3623878656 | bytes 15000000 | tf_op jit(solution)/shard_map/product/pallas_call | solution.py:52
  90.4 1.3 copy-done.1
  91.6 1.3 copy-done.3
  92.9 1.9 relay.1
  94.8 1.9 collective-permute-start.7
  96.7 4.6 %collective-permute-start.8 = (bf16[2,4,2,32,768]{4,3,2,1,0:T(8,128)(2,1)}, bf16[2,4,2,32,768]{4,3,2,1,0:T(8,128)(2,1)}, u32[]{:S(2)}, u32[]{:S(2)}) collective-permute-start(bf16[2,4,2,32,768]{4,3,2,1,0:T(8,128)(2,1)} %get-tuple-element.37), channel_id=1, source_target_pairs={{0,3},{1,0},{2,1},{3,2},{4,7},{5,4},{6,5},{7,6},{8,11},{9,8},{10,9... | collective-permute-start | bytes 2359304 | tf_op jit(solution)/shard_map/ppermute | solution.py:318
  101.3 15.0 %collective-permute-done.7.low = bf16[2,4,2,32,768]{4,3,2,1,0:T(8,128)(2,1)S(1)} collective-permute-done((bf16[2,4,2,32,768]{4,3,2,1,0:T(8,128)(2,1)}, bf16[2,4,2,32,768]{4,3,2,1,0:T(8,128)(2,1)S(1)}, u32[]{:S(2)}, u32[]{:S(2)}) %collective-permute-start.7) | collective-permute-done | bytes 786464 | tf_op jit(solution)/shard_map/ppermute | solution.py:318
  116.3 0.9 collective-permute-done.8.high
  117.2 2.3 %sum_x.1 = bf16[4,2,2,32,768]{4,3,2,1,0:T(8,128)(2,1)S(1)} custom-call(s32[1]{0:T(128)} %bitcast.yl, bf16[3,4,2,32,768]{4,3,2,1,0:T(8,128)(2,1)S(1)} %copy-done.2, bf16[3,4,2,32,768]{4,3,2,1,0:T(8,128)(2,1)S(1)} %copy-done.4, bf16[2,4,2,32,768]{4,3,2,1,0:T(8,128)(2,1)S(1)} %collective-permute-done.7.low, bf16[2,4,2,32,768]{4,3,2,1,0:T(8,128)(2,1)} %collective-permute-done.8.high), custom_call_target="tpu_custom_call" | custom-call | tf_op jit(solution)/shard_map/sum_x/pallas_call | solution.py:109
  119.5 31.4 %all_to_all.25 = bf16[8,64,768]{2,1,0:T(8,128)(2,1)S(1)} all-to-all(bf16[8,64,768]{2,1,0:T(8,128)(2,1)S(1)} %bitcast.29), channel_id=1, replica_groups=mesh['z'=8,'yl'=2,'c'=2,'yh'=4,'x'=4] {'yh','yl'}, dimensions={0} | all-to-all | bytes 1572864 | tf_op jit(solution)/shard_map/all_to_all | solution.py:361
  150.9 0.7 features.1
  151.6 2.6 %collective-permute-start.9 = (f32[2,64,128]{2,1,0:T(8,128)S(1)}, f32[2,64,128]{2,1,0:T(8,128)S(1)}, u32[]{:S(2)}, u32[]{:S(2)}) collective-permute-start(f32[2,64,128]{2,1,0:T(8,128)S(1)} %get-tuple-element.40.mine), channel_id=1, source_target_pairs={{0,16},{16,0},{1,17},{17,1},{2,18},{18,2},{3,19},{19,3},{4,20},{20... | collective-permute-start | bytes 196616 | tf_op jit(solution)/shard_map/ppermute | solution.py:365
  154.2 3.1 %fusion.6.pred = f32[64,1536]{1,0:T(8,128)S(1)} fusion(bf16[64,1024]{1,0:T(8,128)(2,1)S(1)} %bitcast.35, bf16[1536,1024]{1,0:T(8,128)(2,1)} %bitcast.37), kind=kOutput, calls=%fused_computation.16 | convolution fusion | flops 201326592 | bytes 3670016 | tf_op jit(solution)/shard_map/dot_general | solution.py:26
  157.6 15.9 %all_to_all.26 = bf16[16,64,96]{2,1,0:T(8,128)(2,1)S(1)} all-to-all(bf16[16,64,96]{2,1,0:T(8,128)(2,1)S(1)} %get-tuple-element.44), channel_id=1, replica_groups=mesh['z'=8,'yl'=2,'c'=2,'yh'=4,'x'=4] {'yh','x'}, dimensions={0} | all-to-all | bytes 393216 | tf_op jit(solution)/shard_map/all_to_all | solution.py:367
  173.5 1.4 grad_part.1
  175.0 8.9 %all-to-all-start.3 = ((bf16[16,48,128]{2,1,0:T(8,128)(2,1)}), bf16[16,48,128]{2,1,0:T(8,128)(2,1)S(1)}, u32[]{:S(2)}, u32[]{:S(2)}) async-start(bf16[16,48,128]{2,1,0:T(8,128)(2,1)} %grad_part.1), calls=%async_computation.3 | async-start | bytes 393216 | tf_op jit(solution)/shard_map/all_to_all | solution.py:369
  183.9 2.6 %fusion.7 = f32[64,1024]{1,0:T(8,128)S(1)} fusion(bf16[64,1536]{1,0:T(8,128)(2,1)S(1)} %get-tuple-element.43, bf16[1536,1024]{1,0:T(8,128)(2,1)} %bitcast.38), kind=kOutput, calls=%fused_computation.17 | convolution fusion | flops 201326592 | bytes 3604480 | tf_op jit(solution)/shard_map/dot_general | solution.py:373
  186.5 2.9 %collective-permute-start.10 = (bf16[32,1024]{1,0:T(8,128)(2,1)S(1)}, bf16[32,1024]{1,0:T(8,128)(2,1)S(1)}, u32[]{:S(2)}, u32[]{:S(2)}) collective-permute-start(bf16[32,1024]{1,0:T(8,128)(2,1)S(1)} %slice.19), channel_id=1, source_target_pairs={{0,16},{16,0},{1,17},{17,1},{2,18},{18,2},{3,19},{19,3},{4,20},{20... | collective-permute-start | bytes 196616 | tf_op jit(solution)/shard_map/ppermute | solution.py:374
  189.4 3.2 %all-to-all-done.3.got = bf16[16,48,128]{2,1,0:T(8,128)(2,1)S(1)} async-done(((bf16[16,48,128]{2,1,0:T(8,128)(2,1)}), bf16[16,48,128]{2,1,0:T(8,128)(2,1)S(1)}, u32[]{:S(2)}, u32[]{:S(2)}) %all-to-all-start.3) | async-done | bytes 196640 | tf_op jit(solution)/shard_map/all_to_all | solution.py:369
  192.5 0.7 sum_grad.1
  193.3 4.7 %all-to-all-start.4 = ((bf16[16,48,128]{2,1,0:T(8,128)(2,1)}), bf16[16,48,128]{2,1,0:T(8,128)(2,1)S(1)}, u32[]{:S(2)}, u32[]{:S(2)}) async-start(bf16[16,48,128]{2,1,0:T(8,128)(2,1)} %sum_grad.1), calls=%async_computation.4 | async-start | bytes 393216 | tf_op jit(solution)/shard_map/all_to_all | solution.py:370
  198.0 1.0 fusion.1
  199.0 7.6 %all-to-all-done.4.mine = bf16[16,48,128]{2,1,0:T(8,128)(2,1)S(1)} async-done(((bf16[16,48,128]{2,1,0:T(8,128)(2,1)}), bf16[16,48,128]{2,1,0:T(8,128)(2,1)S(1)}, u32[]{:S(2)}, u32[]{:S(2)}) %all-to-all-start.4) | async-done | bytes 196640 | tf_op jit(solution)/shard_map/all_to_all | solution.py:370
  206.6 4.5 %collective-permute-start.11 = (bf16[16,48,128]{2,1,0:T(8,128)(2,1)S(1)}, bf16[16,48,128]{2,1,0:T(8,128)(2,1)S(1)}, u32[]{:S(2)}, u32[]{:S(2)}) collective-permute-start(bf16[16,48,128]{2,1,0:T(8,128)(2,1)S(1)} %all-to-all-done.4.mine), channel_id=1, source_target_pairs={{0,16},{16,0},{1,17},{17,1},{2,18},{18,2},{3,19},{19,3},{4,20},{20... | collective-permute-start | bytes 589832 | tf_op jit(solution)/shard_map/ppermute | solution.py:371
  211.1 1.6 fusion.4
  212.7 0.9 join.1
  (39 shorter events, 1.1 us)
Async XLA Ops:
  7.2 13.4 %copy-start = (bf16[1024,192]{0,1:T(8,128)(2,1)S(1)}, bf16[1024,192]{0,1:T(8,128)(2,1)}, u32[]{:S(2)}) copy-start(bf16[1024,192]{0,1:T(8,128)(2,1)} %param.11) | copy-start | bytes 1179652
  7.2 23.8 %copy-start.7 = (bf16[512,1024]{1,0:T(8,128)(2,1)S(1)}, bf16[512,1024]{1,0:T(8,128)(2,1)}, u32[]{:S(2)}) copy-start(bf16[512,1024]{1,0:T(8,128)(2,1)} %param.9) | copy-start | bytes 3145732
  7.2 18.7 %copy-start.9 = (bf16[32,3072]{1,0:T(8,128)(2,1)S(1)}, bf16[32,3072]{1,0:T(8,128)(2,1)}, u32[]{:S(2)}) copy-start(bf16[32,3072]{1,0:T(8,128)(2,1)} %resid.1) | copy-start | bytes 589828
  7.2 23.8 %copy-start.12 = (f32[1024]{0:T(1024)S(1)}, f32[1024]{0:T(1024)}, u32[]{:S(2)}) copy-start(f32[1024]{0:T(1024)} %param.10) | copy-start | bytes 12292
  7.2 50.3 %all-gather.4.cloned.1.call-start = ((), (), s32[]{:S(2)}) async-start(), calls=%async_computation.5 | async-start | bytes 2654208 | tf_op jit(solution)/shard_map/all_gather | solution.py:332
  7.9 33.5 %collective-permute-start = (bf16[512,1536]{1,0:T(8,128)(2,1)}, bf16[512,1536]{1,0:T(8,128)(2,1)}, u32[]{:S(2)}, u32[]{:S(2)}) collective-permute-start(bf16[512,1536]{1,0:T(8,128)(2,1)} %param.6), channel_id=1, source_target_pairs={{0,32},{32,0},{1,33},{33,1},{2,34},{34,2},{3,35},{35,3},{4,36},{36... | collective-permute-start | bytes 4718600 | tf_op jit(solution)/shard_map/ppermute | solution.py:334
  12.0 29.5 %collective-permute-start.1 = (bf16[512,1536]{1,0:T(8,128)(2,1)}, bf16[512,1536]{1,0:T(8,128)(2,1)}, u32[]{:S(2)}, u32[]{:S(2)}) collective-permute-start(bf16[512,1536]{1,0:T(8,128)(2,1)} %param.6), channel_id=1, source_target_pairs={{0,16},{16,0},{1,17},{17,1},{2,18},{18,2},{3,19},{19,3},{4,20},{20... | collective-permute-start | bytes 4718600 | tf_op jit(solution)/shard_map/ppermute | solution.py:335
  18.7 12.3 %collective-permute-start.3 = (bf16[512,1024]{1,0:T(8,128)(2,1)}, bf16[512,1024]{1,0:T(8,128)(2,1)S(1)}, u32[]{:S(2)}, u32[]{:S(2)}) collective-permute-start(bf16[512,1024]{1,0:T(8,128)(2,1)} %param.9), channel_id=1, source_target_pairs={{0,16},{16,0},{1,17},{17,1},{2,18},{18,2},{3,19},{19,3},{4,20},{20... | collective-permute-start | bytes 3145736 | tf_op jit(solution)/shard_map/ppermute | solution.py:336
  21.6 16.1 %all-to-all-start = ((bf16[4,96,1024]{2,1,0:T(8,128)(2,1)}), bf16[4,96,1024]{2,1,0:T(8,128)(2,1)}, u32[]{:S(2)}, u32[]{:S(2)}) async-start(bf16[4,96,1024]{2,1,0:T(8,128)(2,1)} %broadcast_in_dim.4), calls=%async_computation | async-start | bytes 1572864 | tf_op jit(solution)/shard_map/all_to_all | solution.py:338
  25.8 128.4 %all-gather.6.cloned.1.call-start = ((), (), s32[]{:S(2)}) async-start(), calls=%async_computation.6 | async-start | bytes 3932160 | tf_op jit(solution)/shard_map/all_gather | solution.py:349
  26.9 3.3 %collective-permute-start.2 = (bf16[32,1536]{1,0:T(8,128)(2,1)S(1)}, bf16[32,1536]{1,0:T(8,128)(2,1)S(1)}, u32[]{:S(2)}, u32[]{:S(2)}) collective-permute-start(bf16[32,1536]{1,0:T(8,128)(2,1)S(1)} %get-tuple-element.25), channel_id=1, source_target_pairs={{0,16},{16,0},{1,17},{17,1},{2,18},{18,2},{3,19},{19,3},{4,20},{20... | collective-permute-start | bytes 294920 | tf_op jit(solution)/shard_map/ppermute | solution.py:342
  31.9 1.3 copy-start.5
  33.3 0.6 copy-start.10
  57.6 9.1 %collective-permute-start.4 = (bf16[512,1536]{1,0:T(8,128)(2,1)}, bf16[512,1536]{1,0:T(8,128)(2,1)S(1)}, u32[]{:S(2)}, u32[]{:S(2)}) collective-permute-start(bf16[512,1536]{1,0:T(8,128)(2,1)} %collective-permute-done), channel_id=1, source_target_pairs={{0,16},{16,0},{1,17},{17,1},{2,18},{18,2},{3,19},{19,3},{4,20},{20... | collective-permute-start | bytes 4718600 | tf_op jit(solution)/shard_map/ppermute | solution.py:347
  66.6 1.2 copy-start.13
  72.3 18.1 %collective-permute-start.5 = (bf16[1,4,2,32,768]{4,3,2,1,0:T(8,128)(2,1)}, bf16[1,4,2,32,768]{4,3,2,1,0:T(8,128)(2,1)S(1)}, u32[]{:S(2)}, u32[]{:S(2)}) collective-permute-start(bf16[1,4,2,32,768]{4,3,2,1,0:T(8,128)(2,1)} %get-tuple-element.34), channel_id=1, source_target_pairs={{0,1},{1,2},{2,3},{3,0},{4,5},{5,6},{6,7},{7,4},{8,9},{9,10},{10,1... | collective-permute-start | bytes 1179656 | tf_op jit(solution)/shard_map/ppermute | solution.py:318
  75.4 15.0 %collective-permute-start.6 = (bf16[1,4,2,32,768]{4,3,2,1,0:T(8,128)(2,1)}, bf16[1,4,2,32,768]{4,3,2,1,0:T(8,128)(2,1)S(1)}, u32[]{:S(2)}, u32[]{:S(2)}) collective-permute-start(bf16[1,4,2,32,768]{4,3,2,1,0:T(8,128)(2,1)} %get-tuple-element.35), channel_id=1, source_target_pairs={{0,3},{1,0},{2,1},{3,2},{4,7},{5,4},{6,5},{7,6},{8,11},{9,8},{10,9... | collective-permute-start | bytes 1179656 | tf_op jit(solution)/shard_map/ppermute | solution.py:318
  90.4 1.3 copy-start.1
  91.6 1.3 copy-start.3
  92.9 24.3 %copy-start.2 = (bf16[3,4,2,32,768]{4,3,2,1,0:T(8,128)(2,1)S(1)}, bf16[3,4,2,32,768]{4,3,2,1,0:T(8,128)(2,1)}, u32[]{:S(2)}) copy-start(bf16[3,4,2,32,768]{4,3,2,1,0:T(8,128)(2,1)} %get-tuple-element.32.mine) | copy-start | bytes 3538948
  92.9 24.3 %copy-start.4 = (bf16[3,4,2,32,768]{4,3,2,1,0:T(8,128)(2,1)S(1)}, bf16[3,4,2,32,768]{4,3,2,1,0:T(8,128)(2,1)}, u32[]{:S(2)}) copy-start(bf16[3,4,2,32,768]{4,3,2,1,0:T(8,128)(2,1)} %get-tuple-element.33.rest) | copy-start | bytes 3538948
  94.8 21.5 %collective-permute-start.7 = (bf16[2,4,2,32,768]{4,3,2,1,0:T(8,128)(2,1)}, bf16[2,4,2,32,768]{4,3,2,1,0:T(8,128)(2,1)S(1)}, u32[]{:S(2)}, u32[]{:S(2)}) collective-permute-start(bf16[2,4,2,32,768]{4,3,2,1,0:T(8,128)(2,1)} %get-tuple-element.36), channel_id=1, source_target_pairs={{0,1},{1,2},{2,3},{3,0},{4,5},{5,6},{6,7},{7,4},{8,9},{9,10},{10,1... | collective-permute-start | bytes 2359304 | tf_op jit(solution)/shard_map/ppermute | solution.py:318
  96.7 20.5 %collective-permute-start.8 = (bf16[2,4,2,32,768]{4,3,2,1,0:T(8,128)(2,1)}, bf16[2,4,2,32,768]{4,3,2,1,0:T(8,128)(2,1)}, u32[]{:S(2)}, u32[]{:S(2)}) collective-permute-start(bf16[2,4,2,32,768]{4,3,2,1,0:T(8,128)(2,1)} %get-tuple-element.37), channel_id=1, source_target_pairs={{0,3},{1,0},{2,1},{3,2},{4,7},{5,4},{6,5},{7,6},{8,11},{9,8},{10,9... | collective-permute-start | bytes 2359304 | tf_op jit(solution)/shard_map/ppermute | solution.py:318
  117.2 33.7 %copy-start.8 = (bf16[64,1536]{1,0:T(8,128)(2,1)S(1)}, bf16[64,1536]{1,0:T(8,128)(2,1)}, u32[]{:S(2)}) copy-start(bf16[64,1536]{1,0:T(8,128)(2,1)} %pad_maximum_fusion.resid) | copy-start | bytes 589828
  119.5 34.7 %copy-start.11 = (bf16[2,32,1024]{2,1,0:T(8,128)(2,1)S(1)}, bf16[2,32,1024]{2,1,0:T(8,128)(2,1)}, u32[]{:S(2)}) copy-start(bf16[2,32,1024]{2,1,0:T(8,128)(2,1)} %copy-done.10) | copy-start | bytes 393220
  151.6 5.8 %collective-permute-start.9 = (f32[2,64,128]{2,1,0:T(8,128)S(1)}, f32[2,64,128]{2,1,0:T(8,128)S(1)}, u32[]{:S(2)}, u32[]{:S(2)}) collective-permute-start(f32[2,64,128]{2,1,0:T(8,128)S(1)} %get-tuple-element.40.mine), channel_id=1, source_target_pairs={{0,16},{16,0},{1,17},{17,1},{2,18},{18,2},{3,19},{19,3},{4,20},{20... | collective-permute-start | bytes 196616 | tf_op jit(solution)/shard_map/ppermute | solution.py:365
  154.2 19.3 %copy-start.6 = (bf16[16,2,32,1024]{3,2,1,0:T(8,128)(2,1)S(1)}, bf16[16,2,32,1024]{3,2,1,0:T(8,128)(2,1)}, u32[]{:S(2)}) copy-start(bf16[16,2,32,1024]{3,2,1,0:T(8,128)(2,1)} %copy-done.5) | copy-start | bytes 6291460
  175.0 17.6 %all-to-all-start.3 = ((bf16[16,48,128]{2,1,0:T(8,128)(2,1)}), bf16[16,48,128]{2,1,0:T(8,128)(2,1)S(1)}, u32[]{:S(2)}, u32[]{:S(2)}) async-start(bf16[16,48,128]{2,1,0:T(8,128)(2,1)} %grad_part.1), calls=%async_computation.3 | async-start | bytes 393216 | tf_op jit(solution)/shard_map/all_to_all | solution.py:369
  186.5 11.5 %collective-permute-start.10 = (bf16[32,1024]{1,0:T(8,128)(2,1)S(1)}, bf16[32,1024]{1,0:T(8,128)(2,1)S(1)}, u32[]{:S(2)}, u32[]{:S(2)}) collective-permute-start(bf16[32,1024]{1,0:T(8,128)(2,1)S(1)} %slice.19), channel_id=1, source_target_pairs={{0,16},{16,0},{1,17},{17,1},{2,18},{18,2},{3,19},{19,3},{4,20},{20... | collective-permute-start | bytes 196616 | tf_op jit(solution)/shard_map/ppermute | solution.py:374
  193.3 13.3 %all-to-all-start.4 = ((bf16[16,48,128]{2,1,0:T(8,128)(2,1)}), bf16[16,48,128]{2,1,0:T(8,128)(2,1)S(1)}, u32[]{:S(2)}, u32[]{:S(2)}) async-start(bf16[16,48,128]{2,1,0:T(8,128)(2,1)} %sum_grad.1), calls=%async_computation.4 | async-start | bytes 393216 | tf_op jit(solution)/shard_map/all_to_all | solution.py:370
  206.6 6.1 %collective-permute-start.11 = (bf16[16,48,128]{2,1,0:T(8,128)(2,1)S(1)}, bf16[16,48,128]{2,1,0:T(8,128)(2,1)S(1)}, u32[]{:S(2)}, u32[]{:S(2)}) collective-permute-start(bf16[16,48,128]{2,1,0:T(8,128)(2,1)S(1)} %all-to-all-done.4.mine), channel_id=1, source_target_pairs={{0,16},{16,0},{1,17},{17,1},{2,18},{18,2},{3,19},{19,3},{4,20},{20... | collective-permute-start | bytes 589832 | tf_op jit(solution)/shard_map/ppermute | solution.py:371
Sparse Core Ops, SparseCore 0:
  10.1 47.3 all-gather.3
  59.6 70.2 all-gather.5

commit v3 on v2

--- a/solution.py
+++ b/solution.py
@@ -360,6 +360,7 @@
     send_y = sum_x(yl, mine_parts, rest_parts, low, high).reshape(2 * NYH, 2 * own, cols)
     got_y = lax.all_to_all(send_y, ("yh", "yl"), 0, 0, tiled=True)
     pred = dot_nt(normed_own.reshape(2 * own, width), head_all)
+    got_y, pred = lax.optimization_barrier((got_y, pred))
     feats, stats = features(got_y.reshape(NYH, 2, 2 * own, cols), resid_own)
 
     delta, send_t = deltas(feats, stats, lax.ppermute(stats, "c", SWAP), pred)

time: 222 us -> 221 us (level)
  blocking collectives: 47.3 us -> 15.2 us
  waiting for transfers between devices: 55.1 us -> 73.1 us
  starting transfers between devices: 61.7 us -> 72.3 us
    all_to_all x1 -> x0, blocking collectives: 31.4 us -> none  [local(): got_y = lax.all_to_all(send_y, ('yh', 'yl'), 0, 0, tiled=True)]
    all_to_all x0 -> x1, waiting for transfers between devices: none -> 16.4 us  [local(): got_y = lax.all_to_all(send_y, ('yh', 'yl'), 0, 0, tiled=True)]
    all_to_all x0 -> x1, starting transfers between devices: none -> 6.59 us  [local(): got_y = lax.all_to_all(send_y, ('yh', 'yl'), 0, 0, tiled=True)]
    all_gather x1, waiting for transfers between devices: 0.02 us -> 2.82 us  [local(): head_all = lax.all_gather(head_x, 'yh', axis=0).reshape(2 * cols, width)]
  transfers between devices with their start and end apart: 17 -> 18, of which waited for: 9 -> 12; matrix products, arithmetic and copies ran while one was open for 5% -> 5% of each run, Pallas kernels for 10% -> 11%
where the time goes in v3:
time: 221 us; the launch traced here: 220 us
  waiting for transfers between devices  73.1 us (33%)
  starting transfers between devices  72.3 us (33%)
  Pallas kernels  26.7 us (12%)
  blocking collectives  15.2 us (7%)
  between operations  14.4 us (7%)
  local copies, waits for them, and re-layouts  7.73 us (3%)
  matrix products  6.49 us (3%)
  other arithmetic  3.88 us (2%)
    all_to_all x1, waiting for transfers between devices, local(): got_y = lax.all_to_all(send_y, ('yh', 'yl'), 0, 0, tiled=True)  16.4 us
    all_gather x1, waiting for transfers between devices, local(): w = lax.all_gather(down_w.T, 'z', axis=0, tiled=True)  16.1 us
    ppermute x4, waiting for transfers between devices, send_x(): return lax.ppermute(block, 'x', [(i, (i + step) % NX) for i in range(NX)])  15.9 us
    pallas_call x2, Pallas kernels, product(): pl.pallas_call(product_kernel, grid_spec=pltpu.PrefetchScalarGridSpec(num...  15.4 us
    all_to_all x1, blocking collectives, local(): got_t = lax.all_to_all(send_t, TENSOR, 0, 0, tiled=True)  15.2 us
    ppermute x4, starting transfers between devices, send_x(): return lax.ppermute(block, 'x', [(i, (i + step) % NX) for i in range(NX)])  13 us
    all_to_all x1, starting transfers between devices, local(): got_g = lax.all_to_all(head_part, REPLICA, 0, 0, tiled=True)  8.23 us
    all_to_all x1, waiting for transfers between devices, local(): all_g = lax.all_to_all(sum_grad(got_g), REPLICA, 0, 0, tiled=True)  7.48 us
  transfers between devices with their start and end apart: 18, of which 12 were waited for; matrix products, arithmetic and copies ran while one was open for 5% of the time, Pallas kernels for 11%

profile of v3, /device:TPU:1, one launch (start us, length us, event | category | flops | bytes accessed | tf_op | source)
XLA Modules:
  0.0 219.8 jit_solution(16855846204094251639)
XLA Ops:
  7.9 4.0 %collective-permute-start = (bf16[512,1536]{1,0:T(8,128)(2,1)}, bf16[512,1536]{1,0:T(8,128)(2,1)}, u32[]{:S(2)}, u32[]{:S(2)}) collective-permute-start(bf16[512,1536]{1,0:T(8,128)(2,1)} %param.6), channel_id=1, source_target_pairs={{0,32},{32,0},{1,33},{33,1},{2,34},{34,2},{3,35},{35,3},{4,36},{36... | collective-permute-start | bytes 4718600 | tf_op jit(solution)/shard_map/ppermute | solution.py:334
  12.0 6.7 %collective-permute-start.1 = (bf16[512,1536]{1,0:T(8,128)(2,1)}, bf16[512,1536]{1,0:T(8,128)(2,1)}, u32[]{:S(2)}, u32[]{:S(2)}) collective-permute-start(bf16[512,1536]{1,0:T(8,128)(2,1)} %param.6), channel_id=1, source_target_pairs={{0,16},{16,0},{1,17},{17,1},{2,18},{18,2},{3,19},{19,3},{4,20},{20... | collective-permute-start | bytes 4718600 | tf_op jit(solution)/shard_map/ppermute | solution.py:335
  18.7 1.9 collective-permute-start.3
  20.7 1.0 broadcast_in_dim.4
  21.6 4.2 %all-to-all-start = ((bf16[4,96,1024]{2,1,0:T(8,128)(2,1)}), bf16[4,96,1024]{2,1,0:T(8,128)(2,1)}, u32[]{:S(2)}, u32[]{:S(2)}) async-start(bf16[4,96,1024]{2,1,0:T(8,128)(2,1)} %broadcast_in_dim.4), calls=%async_computation | async-start | bytes 1572864 | tf_op jit(solution)/shard_map/all_to_all | solution.py:338
  25.9 1.1 resid_halves.1
  26.9 2.4 %collective-permute-start.2 = (bf16[32,1536]{1,0:T(8,128)(2,1)S(1)}, bf16[32,1536]{1,0:T(8,128)(2,1)S(1)}, u32[]{:S(2)}, u32[]{:S(2)}) collective-permute-start(bf16[32,1536]{1,0:T(8,128)(2,1)S(1)} %get-tuple-element.27), channel_id=1, source_target_pairs={{0,16},{16,0},{1,17},{17,1},{2,18},{18,2},{3,19},{19,3},{4,20},{20... | collective-permute-start | bytes 294920 | tf_op jit(solution)/shard_map/ppermute | solution.py:342
  29.4 0.9 collective-permute-done.2
  31.0 1.0 norms.1
  32.0 1.3 copy-done.5
  33.9 3.8 %all-to-all-done = bf16[4,96,1024]{2,1,0:T(8,128)(2,1)} async-done(((bf16[4,96,1024]{2,1,0:T(8,128)(2,1)}), bf16[4,96,1024]{2,1,0:T(8,128)(2,1)}, u32[]{:S(2)}, u32[]{:S(2)}) %all-to-all-start) | async-done | bytes 786464 | tf_op jit(solution)/shard_map/all_to_all | solution.py:338
  37.8 3.7 %collective-permute-done = bf16[512,1536]{1,0:T(8,128)(2,1)} collective-permute-done((bf16[512,1536]{1,0:T(8,128)(2,1)}, bf16[512,1536]{1,0:T(8,128)(2,1)}, u32[]{:S(2)}, u32[]{:S(2)}) %collective-permute-start) | collective-permute-done | bytes 1572896 | tf_op jit(solution)/shard_map/ppermute | solution.py:334
  41.5 16.1 %all-gather.4.cloned.1.call-done = bf16[768,1536]{1,0:T(8,128)(2,1)} async-done(((bf16[96,1536]{1,0:T(8,128)(2,1)}), bf16[768,1536]{1,0:T(8,128)(2,1)}) %all-gather.4.cloned.1.call-update) | async-done | bytes 2359312 | tf_op jit(solution)/shard_map/all_gather | solution.py:332
  57.6 5.8 %collective-permute-start.4 = (bf16[512,1536]{1,0:T(8,128)(2,1)}, bf16[512,1536]{1,0:T(8,128)(2,1)S(1)}, u32[]{:S(2)}, u32[]{:S(2)}) collective-permute-start(bf16[512,1536]{1,0:T(8,128)(2,1)} %collective-permute-done), channel_id=1, source_target_pairs={{0,16},{16,0},{1,17},{17,1},{2,18},{18,2},{3,19},{19,3},{4,20},{20... | collective-permute-start | bytes 4718600 | tf_op jit(solution)/shard_map/ppermute | solution.py:347
  63.4 3.2 %collective-permute-done.4 = bf16[512,1536]{1,0:T(8,128)(2,1)S(1)} collective-permute-done((bf16[512,1536]{1,0:T(8,128)(2,1)}, bf16[512,1536]{1,0:T(8,128)(2,1)S(1)}, u32[]{:S(2)}, u32[]{:S(2)}) %collective-permute-start.4) | collective-permute-done | bytes 1572896 | tf_op jit(solution)/shard_map/ppermute | solution.py:347
  66.6 1.2 copy-done.13
  67.8 4.5 %product.3 = (bf16[1,4,2,32,768]{4,3,2,1,0:T(8,128)(2,1)}, bf16[1,4,2,32,768]{4,3,2,1,0:T(8,128)(2,1)}) custom-call(s32[1]{0:T(128)} %bitcast.16.owners, bf16[4,4,32,1536]{3,2,1,0:T(8,128)(2,1)} %bitcast.40, bf16[4,4,32,1536]{3,2,1,0:T(8,128)(2,1)} %bitcast.11.core, bf16[4,4,32,1536]{3,2,1,0:T(8,128)(2,1)} %bitcast.12.other, ...), custom_call_target="tpu_custom_call" | custom-call | flops 1207959552 | bytes 5000000 | tf_op jit(solution)/shard_map/product/pallas_call | solution.py:52
  72.2 3.1 %collective-permute-start.5 = (bf16[1,4,2,32,768]{4,3,2,1,0:T(8,128)(2,1)}, bf16[1,4,2,32,768]{4,3,2,1,0:T(8,128)(2,1)S(1)}, u32[]{:S(2)}, u32[]{:S(2)}) collective-permute-start(bf16[1,4,2,32,768]{4,3,2,1,0:T(8,128)(2,1)} %get-tuple-element.36), channel_id=1, source_target_pairs={{0,1},{1,2},{2,3},{3,0},{4,5},{5,6},{6,7},{7,4},{8,9},{9,10},{10,1... | collective-permute-start | bytes 1179656 | tf_op jit(solution)/shard_map/ppermute | solution.py:318
  75.3 3.4 %collective-permute-start.6 = (bf16[1,4,2,32,768]{4,3,2,1,0:T(8,128)(2,1)}, bf16[1,4,2,32,768]{4,3,2,1,0:T(8,128)(2,1)S(1)}, u32[]{:S(2)}, u32[]{:S(2)}) collective-permute-start(bf16[1,4,2,32,768]{4,3,2,1,0:T(8,128)(2,1)} %get-tuple-element.37), channel_id=1, source_target_pairs={{0,3},{1,0},{2,1},{3,2},{4,7},{5,4},{6,5},{7,6},{8,11},{9,8},{10,9... | collective-permute-start | bytes 1179656 | tf_op jit(solution)/shard_map/ppermute | solution.py:318
  79.3 10.9 %product.2 = (bf16[3,4,2,32,768]{4,3,2,1,0:T(8,128)(2,1)}, bf16[3,4,2,32,768]{4,3,2,1,0:T(8,128)(2,1)}) custom-call(s32[3]{0:T(128)} %pad_add_fusion.owners, bf16[4,4,32,1536]{3,2,1,0:T(8,128)(2,1)} %bitcast.41, bf16[4,4,32,1536]{3,2,1,0:T(8,128)(2,1)} %bitcast.11.core, bf16[4,4,32,1536]{3,2,1,0:T(8,128)(2,1)} %bitcast.12.other, ...), custom_call_target="tpu_custom_call" | custom-call | flops 3623878656 | bytes 15000000 | tf_op jit(solution)/shard_map/product/pallas_call | solution.py:52
  90.3 1.3 copy-done.1
  91.6 1.3 copy-done.3
  92.8 1.8 relay.1
  94.7 1.9 collective-permute-start.7
  96.6 4.6 %collective-permute-start.8 = (bf16[2,4,2,32,768]{4,3,2,1,0:T(8,128)(2,1)}, bf16[2,4,2,32,768]{4,3,2,1,0:T(8,128)(2,1)}, u32[]{:S(2)}, u32[]{:S(2)}) collective-permute-start(bf16[2,4,2,32,768]{4,3,2,1,0:T(8,128)(2,1)} %get-tuple-element.39), channel_id=1, source_target_pairs={{0,3},{1,0},{2,1},{3,2},{4,7},{5,4},{6,5},{7,6},{8,11},{9,8},{10,9... | collective-permute-start | bytes 2359304 | tf_op jit(solution)/shard_map/ppermute | solution.py:318
  101.2 15.0 %collective-permute-done.7.low = bf16[2,4,2,32,768]{4,3,2,1,0:T(8,128)(2,1)S(1)} collective-permute-done((bf16[2,4,2,32,768]{4,3,2,1,0:T(8,128)(2,1)}, bf16[2,4,2,32,768]{4,3,2,1,0:T(8,128)(2,1)S(1)}, u32[]{:S(2)}, u32[]{:S(2)}) %collective-permute-start.7) | collective-permute-done | bytes 786464 | tf_op jit(solution)/shard_map/ppermute | solution.py:318
  116.2 0.9 collective-permute-done.8.high
  117.1 3.4 %sum_x.1 = bf16[4,2,2,32,768]{4,3,2,1,0:T(8,128)(2,1)} custom-call(s32[1]{0:T(128)} %bitcast.yl, bf16[3,4,2,32,768]{4,3,2,1,0:T(8,128)(2,1)S(1)} %copy-done.2, bf16[3,4,2,32,768]{4,3,2,1,0:T(8,128)(2,1)S(1)} %copy-done.4, bf16[2,4,2,32,768]{4,3,2,1,0:T(8,128)(2,1)S(1)} %collective-permute-done.7.low, bf16[2,4,2,32,768]{4,3,2,1,0:T(8,128)(2,1)} %collective-permute-done.8.high), custom_call_target="tpu_custom_call" | custom-call | tf_op jit(solution)/shard_map/sum_x/pallas_call | solution.py:109
  120.5 6.6 %all-to-all-start.1 = ((bf16[8,64,768]{2,1,0:T(8,128)(2,1)}), bf16[8,64,768]{2,1,0:T(8,128)(2,1)S(1)}, u32[]{:S(2)}, u32[]{:S(2)}) async-start(bf16[8,64,768]{2,1,0:T(8,128)(2,1)} %bitcast.17), calls=%async_computation.1 | async-start | bytes 1572864 | tf_op jit(solution)/shard_map/all_to_all | solution.py:361
  127.1 2.8 %all-gather.6.cloned.1.call-done = bf16[16,96,1024]{2,1,0:T(8,128)(2,1)} async-done(((bf16[4,96,1024]{2,1,0:T(8,128)(2,1)}), bf16[16,96,1024]{2,1,0:T(8,128)(2,1)}) %all-gather.6.cloned.1.call-update) | async-done | bytes 3145744 | tf_op jit(solution)/shard_map/all_gather | solution.py:349
  130.0 3.9 %fusion.6.pred = f32[64,1536]{1,0:T(8,128)} fusion(bf16[64,1024]{1,0:T(8,128)(2,1)} %bitcast.34, bf16[1536,1024]{1,0:T(8,128)(2,1)} %bitcast.36), kind=kOutput, calls=%fused_computation.16 | convolution fusion | flops 201326592 | bytes 3670016 | tf_op jit(solution)/shard_map/dot_general | solution.py:26
  133.9 16.4 %all-to-all-done.1 = bf16[8,64,768]{2,1,0:T(8,128)(2,1)S(1)} async-done(((bf16[8,64,768]{2,1,0:T(8,128)(2,1)}), bf16[8,64,768]{2,1,0:T(8,128)(2,1)S(1)}, u32[]{:S(2)}, u32[]{:S(2)}) %all-to-all-start.1) | async-done | bytes 786464 | tf_op jit(solution)/shard_map/all_to_all | solution.py:361
  151.0 3.2 %collective-permute-start.9 = (f32[2,64,128]{2,1,0:T(8,128)S(1)}, f32[2,64,128]{2,1,0:T(8,128)S(1)}, u32[]{:S(2)}, u32[]{:S(2)}) collective-permute-start(f32[2,64,128]{2,1,0:T(8,128)S(1)} %get-tuple-element.45.mine), channel_id=1, source_target_pairs={{0,16},{16,0},{1,17},{17,1},{2,18},{18,2},{3,19},{19,3},{4,20},{20... | collective-permute-start | bytes 196616 | tf_op jit(solution)/shard_map/ppermute | solution.py:366
  154.2 0.9 collective-permute-done.9.other
  155.1 1.0 copy-done.7
  156.3 15.2 %all_to_all.25 = bf16[16,64,96]{2,1,0:T(8,128)(2,1)S(1)} all-to-all(bf16[16,64,96]{2,1,0:T(8,128)(2,1)S(1)} %get-tuple-element.48), channel_id=1, replica_groups=mesh['z'=8,'yl'=2,'c'=2,'yh'=4,'x'=4] {'yh','x'}, dimensions={0} | all-to-all | bytes 393216 | tf_op jit(solution)/shard_map/all_to_all | solution.py:368
  171.6 1.4 grad_part.1
  173.0 8.2 %all-to-all-start.3 = ((bf16[16,48,128]{2,1,0:T(8,128)(2,1)}), bf16[16,48,128]{2,1,0:T(8,128)(2,1)S(1)}, u32[]{:S(2)}, u32[]{:S(2)}) async-start(bf16[16,48,128]{2,1,0:T(8,128)(2,1)} %grad_part.1), calls=%async_computation.3 | async-start | bytes 393216 | tf_op jit(solution)/shard_map/all_to_all | solution.py:370
  181.2 2.6 %fusion.7 = f32[64,1024]{1,0:T(8,128)S(1)} fusion(bf16[64,1536]{1,0:T(8,128)(2,1)S(1)} %get-tuple-element.47, bf16[1536,1024]{1,0:T(8,128)(2,1)} %bitcast.37), kind=kOutput, calls=%fused_computation.17 | convolution fusion | flops 201326592 | bytes 3604480 | tf_op jit(solution)/shard_map/dot_general | solution.py:374
  183.8 4.9 %collective-permute-start.10 = (bf16[32,1024]{1,0:T(8,128)(2,1)S(1)}, bf16[32,1024]{1,0:T(8,128)(2,1)S(1)}, u32[]{:S(2)}, u32[]{:S(2)}) collective-permute-start(bf16[32,1024]{1,0:T(8,128)(2,1)S(1)} %slice.19), channel_id=1, source_target_pairs={{0,16},{16,0},{1,17},{17,1},{2,18},{18,2},{3,19},{19,3},{4,20},{20... | collective-permute-start | bytes 196616 | tf_op jit(solution)/shard_map/ppermute | solution.py:375
  188.8 1.2 all-to-all-done.3.got
  189.9 0.7 sum_grad.1
  190.6 6.7 %all-to-all-start.4 = ((bf16[16,48,128]{2,1,0:T(8,128)(2,1)}), bf16[16,48,128]{2,1,0:T(8,128)(2,1)S(1)}, u32[]{:S(2)}, u32[]{:S(2)}) async-start(bf16[16,48,128]{2,1,0:T(8,128)(2,1)} %sum_grad.1), calls=%async_computation.4 | async-start | bytes 393216 | tf_op jit(solution)/shard_map/all_to_all | solution.py:371
  197.3 1.0 fusion.1
  198.3 7.5 %all-to-all-done.4.mine = bf16[16,48,128]{2,1,0:T(8,128)(2,1)S(1)} async-done(((bf16[16,48,128]{2,1,0:T(8,128)(2,1)}), bf16[16,48,128]{2,1,0:T(8,128)(2,1)S(1)}, u32[]{:S(2)}, u32[]{:S(2)}) %all-to-all-start.4) | async-done | bytes 196640 | tf_op jit(solution)/shard_map/all_to_all | solution.py:371
  205.8 4.6 %collective-permute-start.11 = (bf16[16,48,128]{2,1,0:T(8,128)(2,1)S(1)}, bf16[16,48,128]{2,1,0:T(8,128)(2,1)S(1)}, u32[]{:S(2)}, u32[]{:S(2)}) collective-permute-start(bf16[16,48,128]{2,1,0:T(8,128)(2,1)S(1)} %all-to-all-done.4.mine), channel_id=1, source_target_pairs={{0,16},{16,0},{1,17},{17,1},{2,18},{18,2},{3,19},{19,3},{4,20},{20... | collective-permute-start | bytes 589832 | tf_op jit(solution)/shard_map/ppermute | solution.py:372
  210.4 1.6 fusion.4
  212.0 0.9 join.1
  (40 shorter events, 3.8 us)
Async XLA Ops:
  7.2 13.4 %copy-start = (bf16[1024,192]{0,1:T(8,128)(2,1)S(1)}, bf16[1024,192]{0,1:T(8,128)(2,1)}, u32[]{:S(2)}) copy-start(bf16[1024,192]{0,1:T(8,128)(2,1)} %param.11) | copy-start | bytes 1179652
  7.2 23.8 %copy-start.8 = (bf16[512,1024]{1,0:T(8,128)(2,1)S(1)}, bf16[512,1024]{1,0:T(8,128)(2,1)}, u32[]{:S(2)}) copy-start(bf16[512,1024]{1,0:T(8,128)(2,1)} %param.9) | copy-start | bytes 3145732
  7.2 18.7 %copy-start.10 = (bf16[32,3072]{1,0:T(8,128)(2,1)S(1)}, bf16[32,3072]{1,0:T(8,128)(2,1)}, u32[]{:S(2)}) copy-start(bf16[32,3072]{1,0:T(8,128)(2,1)} %resid.1) | copy-start | bytes 589828
  7.2 23.8 %copy-start.12 = (f32[1024]{0:T(1024)S(1)}, f32[1024]{0:T(1024)}, u32[]{:S(2)}) copy-start(f32[1024]{0:T(1024)} %param.10) | copy-start | bytes 12292
  7.2 50.3 %all-gather.4.cloned.1.call-start = ((), (), s32[]{:S(2)}) async-start(), calls=%async_computation.5 | async-start | bytes 2654208 | tf_op jit(solution)/shard_map/all_gather | solution.py:332
  7.9 33.5 %collective-permute-start = (bf16[512,1536]{1,0:T(8,128)(2,1)}, bf16[512,1536]{1,0:T(8,128)(2,1)}, u32[]{:S(2)}, u32[]{:S(2)}) collective-permute-start(bf16[512,1536]{1,0:T(8,128)(2,1)} %param.6), channel_id=1, source_target_pairs={{0,32},{32,0},{1,33},{33,1},{2,34},{34,2},{3,35},{35,3},{4,36},{36... | collective-permute-start | bytes 4718600 | tf_op jit(solution)/shard_map/ppermute | solution.py:334
  12.0 29.5 %collective-permute-start.1 = (bf16[512,1536]{1,0:T(8,128)(2,1)}, bf16[512,1536]{1,0:T(8,128)(2,1)}, u32[]{:S(2)}, u32[]{:S(2)}) collective-permute-start(bf16[512,1536]{1,0:T(8,128)(2,1)} %param.6), channel_id=1, source_target_pairs={{0,16},{16,0},{1,17},{17,1},{2,18},{18,2},{3,19},{19,3},{4,20},{20... | collective-permute-start | bytes 4718600 | tf_op jit(solution)/shard_map/ppermute | solution.py:335
  18.7 12.3 %collective-permute-start.3 = (bf16[512,1024]{1,0:T(8,128)(2,1)}, bf16[512,1024]{1,0:T(8,128)(2,1)S(1)}, u32[]{:S(2)}, u32[]{:S(2)}) collective-permute-start(bf16[512,1024]{1,0:T(8,128)(2,1)} %param.9), channel_id=1, source_target_pairs={{0,16},{16,0},{1,17},{17,1},{2,18},{18,2},{3,19},{19,3},{4,20},{20... | collective-permute-start | bytes 3145736 | tf_op jit(solution)/shard_map/ppermute | solution.py:336
  21.6 16.1 %all-to-all-start = ((bf16[4,96,1024]{2,1,0:T(8,128)(2,1)}), bf16[4,96,1024]{2,1,0:T(8,128)(2,1)}, u32[]{:S(2)}, u32[]{:S(2)}) async-start(bf16[4,96,1024]{2,1,0:T(8,128)(2,1)} %broadcast_in_dim.4), calls=%async_computation | async-start | bytes 1572864 | tf_op jit(solution)/shard_map/all_to_all | solution.py:338
  25.8 104.1 %all-gather.6.cloned.1.call-start = ((), (), s32[]{:S(2)}) async-start(), calls=%async_computation.6 | async-start | bytes 3932160 | tf_op jit(solution)/shard_map/all_gather | solution.py:349
  26.9 3.3 %collective-permute-start.2 = (bf16[32,1536]{1,0:T(8,128)(2,1)S(1)}, bf16[32,1536]{1,0:T(8,128)(2,1)S(1)}, u32[]{:S(2)}, u32[]{:S(2)}) collective-permute-start(bf16[32,1536]{1,0:T(8,128)(2,1)S(1)} %get-tuple-element.27), channel_id=1, source_target_pairs={{0,16},{16,0},{1,17},{17,1},{2,18},{18,2},{3,19},{19,3},{4,20},{20... | collective-permute-start | bytes 294920 | tf_op jit(solution)/shard_map/ppermute | solution.py:342
  32.0 1.3 copy-start.5
  33.3 0.6 copy-start.11
  57.6 9.0 %collective-permute-start.4 = (bf16[512,1536]{1,0:T(8,128)(2,1)}, bf16[512,1536]{1,0:T(8,128)(2,1)S(1)}, u32[]{:S(2)}, u32[]{:S(2)}) collective-permute-start(bf16[512,1536]{1,0:T(8,128)(2,1)} %collective-permute-done), channel_id=1, source_target_pairs={{0,16},{16,0},{1,17},{17,1},{2,18},{18,2},{3,19},{19,3},{4,20},{20... | collective-permute-start | bytes 4718600 | tf_op jit(solution)/shard_map/ppermute | solution.py:347
  66.6 1.2 copy-start.13
  72.2 18.0 %collective-permute-start.5 = (bf16[1,4,2,32,768]{4,3,2,1,0:T(8,128)(2,1)}, bf16[1,4,2,32,768]{4,3,2,1,0:T(8,128)(2,1)S(1)}, u32[]{:S(2)}, u32[]{:S(2)}) collective-permute-start(bf16[1,4,2,32,768]{4,3,2,1,0:T(8,128)(2,1)} %get-tuple-element.36), channel_id=1, source_target_pairs={{0,1},{1,2},{2,3},{3,0},{4,5},{5,6},{6,7},{7,4},{8,9},{9,10},{10,1... | collective-permute-start | bytes 1179656 | tf_op jit(solution)/shard_map/ppermute | solution.py:318
  75.3 15.0 %collective-permute-start.6 = (bf16[1,4,2,32,768]{4,3,2,1,0:T(8,128)(2,1)}, bf16[1,4,2,32,768]{4,3,2,1,0:T(8,128)(2,1)S(1)}, u32[]{:S(2)}, u32[]{:S(2)}) collective-permute-start(bf16[1,4,2,32,768]{4,3,2,1,0:T(8,128)(2,1)} %get-tuple-element.37), channel_id=1, source_target_pairs={{0,3},{1,0},{2,1},{3,2},{4,7},{5,4},{6,5},{7,6},{8,11},{9,8},{10,9... | collective-permute-start | bytes 1179656 | tf_op jit(solution)/shard_map/ppermute | solution.py:318
  90.3 1.3 copy-start.1
  91.6 1.3 copy-start.3
  92.8 24.3 %copy-start.2 = (bf16[3,4,2,32,768]{4,3,2,1,0:T(8,128)(2,1)S(1)}, bf16[3,4,2,32,768]{4,3,2,1,0:T(8,128)(2,1)}, u32[]{:S(2)}) copy-start(bf16[3,4,2,32,768]{4,3,2,1,0:T(8,128)(2,1)} %get-tuple-element.34.mine) | copy-start | bytes 3538948
  92.8 24.3 %copy-start.4 = (bf16[3,4,2,32,768]{4,3,2,1,0:T(8,128)(2,1)S(1)}, bf16[3,4,2,32,768]{4,3,2,1,0:T(8,128)(2,1)}, u32[]{:S(2)}) copy-start(bf16[3,4,2,32,768]{4,3,2,1,0:T(8,128)(2,1)} %get-tuple-element.35.rest) | copy-start | bytes 3538948
  94.7 21.5 %collective-permute-start.7 = (bf16[2,4,2,32,768]{4,3,2,1,0:T(8,128)(2,1)}, bf16[2,4,2,32,768]{4,3,2,1,0:T(8,128)(2,1)S(1)}, u32[]{:S(2)}, u32[]{:S(2)}) collective-permute-start(bf16[2,4,2,32,768]{4,3,2,1,0:T(8,128)(2,1)} %get-tuple-element.38), channel_id=1, source_target_pairs={{0,1},{1,2},{2,3},{3,0},{4,5},{5,6},{6,7},{7,4},{8,9},{9,10},{10,1... | collective-permute-start | bytes 2359304 | tf_op jit(solution)/shard_map/ppermute | solution.py:318
  96.6 20.5 %collective-permute-start.8 = (bf16[2,4,2,32,768]{4,3,2,1,0:T(8,128)(2,1)}, bf16[2,4,2,32,768]{4,3,2,1,0:T(8,128)(2,1)}, u32[]{:S(2)}, u32[]{:S(2)}) collective-permute-start(bf16[2,4,2,32,768]{4,3,2,1,0:T(8,128)(2,1)} %get-tuple-element.39), channel_id=1, source_target_pairs={{0,3},{1,0},{2,1},{3,2},{4,7},{5,4},{6,5},{7,6},{8,11},{9,8},{10,9... | collective-permute-start | bytes 2359304 | tf_op jit(solution)/shard_map/ppermute | solution.py:318
  120.5 29.7 %copy-start.9 = (bf16[64,1536]{1,0:T(8,128)(2,1)S(1)}, bf16[64,1536]{1,0:T(8,128)(2,1)}, u32[]{:S(2)}) copy-start(bf16[64,1536]{1,0:T(8,128)(2,1)} %pad_maximum_fusion.resid) | copy-start | bytes 589828
  120.5 29.7 %all-to-all-start.1 = ((bf16[8,64,768]{2,1,0:T(8,128)(2,1)}), bf16[8,64,768]{2,1,0:T(8,128)(2,1)S(1)}, u32[]{:S(2)}, u32[]{:S(2)}) async-start(bf16[8,64,768]{2,1,0:T(8,128)(2,1)} %bitcast.17), calls=%async_computation.1 | async-start | bytes 1572864 | tf_op jit(solution)/shard_map/all_to_all | solution.py:361
  129.9 41.6 %copy-start.6 = (bf16[16,2,32,1024]{3,2,1,0:T(8,128)(2,1)S(1)}, bf16[16,2,32,1024]{3,2,1,0:T(8,128)(2,1)}, u32[]{:S(2)}) copy-start(bf16[16,2,32,1024]{3,2,1,0:T(8,128)(2,1)} %copy-done.5) | copy-start | bytes 6291460
  151.0 4.1 %collective-permute-start.9 = (f32[2,64,128]{2,1,0:T(8,128)S(1)}, f32[2,64,128]{2,1,0:T(8,128)S(1)}, u32[]{:S(2)}, u32[]{:S(2)}) collective-permute-start(f32[2,64,128]{2,1,0:T(8,128)S(1)} %get-tuple-element.45.mine), channel_id=1, source_target_pairs={{0,16},{16,0},{1,17},{17,1},{2,18},{18,2},{3,19},{19,3},{4,20},{20... | collective-permute-start | bytes 196616 | tf_op jit(solution)/shard_map/ppermute | solution.py:366
  155.1 1.0 copy-start.7
  173.0 16.9 %all-to-all-start.3 = ((bf16[16,48,128]{2,1,0:T(8,128)(2,1)}), bf16[16,48,128]{2,1,0:T(8,128)(2,1)S(1)}, u32[]{:S(2)}, u32[]{:S(2)}) async-start(bf16[16,48,128]{2,1,0:T(8,128)(2,1)} %grad_part.1), calls=%async_computation.3 | async-start | bytes 393216 | tf_op jit(solution)/shard_map/all_to_all | solution.py:370
  183.8 13.5 %collective-permute-start.10 = (bf16[32,1024]{1,0:T(8,128)(2,1)S(1)}, bf16[32,1024]{1,0:T(8,128)(2,1)S(1)}, u32[]{:S(2)}, u32[]{:S(2)}) collective-permute-start(bf16[32,1024]{1,0:T(8,128)(2,1)S(1)} %slice.19), channel_id=1, source_target_pairs={{0,16},{16,0},{1,17},{17,1},{2,18},{18,2},{3,19},{19,3},{4,20},{20... | collective-permute-start | bytes 196616 | tf_op jit(solution)/shard_map/ppermute | solution.py:375
  190.6 15.2 %all-to-all-start.4 = ((bf16[16,48,128]{2,1,0:T(8,128)(2,1)}), bf16[16,48,128]{2,1,0:T(8,128)(2,1)S(1)}, u32[]{:S(2)}, u32[]{:S(2)}) async-start(bf16[16,48,128]{2,1,0:T(8,128)(2,1)} %sum_grad.1), calls=%async_computation.4 | async-start | bytes 393216 | tf_op jit(solution)/shard_map/all_to_all | solution.py:371
  205.8 6.2 %collective-permute-start.11 = (bf16[16,48,128]{2,1,0:T(8,128)(2,1)S(1)}, bf16[16,48,128]{2,1,0:T(8,128)(2,1)S(1)}, u32[]{:S(2)}, u32[]{:S(2)}) collective-permute-start(bf16[16,48,128]{2,1,0:T(8,128)(2,1)S(1)} %all-to-all-done.4.mine), channel_id=1, source_target_pairs={{0,16},{16,0},{1,17},{17,1},{2,18},{18,2},{3,19},{19,3},{4,20},{20... | collective-permute-start | bytes 589832 | tf_op jit(solution)/shard_map/ppermute | solution.py:372
Sparse Core Ops, SparseCore 0:
  10.1 47.3 all-gather.3
  59.6 70.2 all-gather.5

commit v4 on v3

--- a/solution.py
+++ b/solution.py
@@ -345,7 +345,7 @@
         (hidden_y, hidden_c, head_x, resid_own, normed, normed_own)
     )
     hidden_yc = lax.ppermute(hidden_y, "c", SWAP)
-    w, head_x = lax.optimization_barrier((w, head_x))
+    w, head_x, hidden_yc = lax.optimization_barrier((w, head_x, hidden_yc))
     head_all = lax.all_gather(head_x, "yh", axis=0).reshape(2 * cols, width)
 
     x = lax.axis_index("x").astype(jnp.int32)

time: 221 us -> 223 us (level)
  starting transfers between devices: 72.3 us -> 76.5 us
  waiting for transfers between devices: 73.1 us -> 69.3 us
    all_gather x1, waiting for transfers between devices: 2.82 us -> 28.2 us  [local(): head_all = lax.all_gather(head_x, 'yh', axis=0).reshape(2 * cols, width)]
    all_to_all x1, waiting for transfers between devices: 16.4 us -> 0.51 us  [local(): got_y = lax.all_to_all(send_y, ('yh', 'yl'), 0, 0, tiled=True)]
    all_gather x1, waiting for transfers between devices: 16.1 us -> 4.77 us  [local(): w = lax.all_gather(down_w.T, 'z', axis=0, tiled=True)]
    ppermute x1, starting transfers between devices: 3.22 us -> 6.82 us  [local(): delta, send_t = deltas(feats, stats, lax.ppermute(stats, 'c', SWAP), pred)]
    ppermute x4, waiting for transfers between devices: 15.9 us -> 12.4 us  [send_x(): return lax.ppermute(block, 'x', [(i, (i + step) % NX) for i in range(NX)])]
    ppermute x1, starting transfers between devices: 5.8 us -> 8.05 us  [local(): hidden_yc = lax.ppermute(hidden_y, 'c', SWAP)]
where the time goes in v4:
time: 223 us; the launch traced here: 221 us
  starting transfers between devices  76.5 us (34%)
  waiting for transfers between devices  69.3 us (31%)
  Pallas kernels  27.1 us (12%)
  blocking collectives  17.2 us (8%)
  between operations  14.4 us (6%)
  local copies, waits for them, and re-layouts  6.55 us (3%)
  matrix products  6.5 us (3%)
  other arithmetic  3.88 us (2%)
    all_gather x1, waiting for transfers between devices, local(): head_all = lax.all_gather(head_x, 'yh', axis=0).reshape(2 * cols, width)  28.2 us
    all_to_all x1, blocking collectives, local(): got_t = lax.all_to_all(send_t, TENSOR, 0, 0, tiled=True)  17.2 us
    pallas_call x2, Pallas kernels, product(): pl.pallas_call(product_kernel, grid_spec=pltpu.PrefetchScalarGridSpec(num...  15.8 us
    ppermute x4, starting transfers between devices, send_x(): return lax.ppermute(block, 'x', [(i, (i + step) % NX) for i in range(NX)])  13 us
    ppermute x4, waiting for transfers between devices, send_x(): return lax.ppermute(block, 'x', [(i, (i + step) % NX) for i in range(NX)])  12.4 us
    all_to_all x1, starting transfers between devices, local(): got_g = lax.all_to_all(head_part, REPLICA, 0, 0, tiled=True)  9.35 us
    ppermute x1, starting transfers between devices, local(): hidden_yc = lax.ppermute(hidden_y, 'c', SWAP)  8.05 us
    all_to_all x1, waiting for transfers between devices, local(): all_g = lax.all_to_all(sum_grad(got_g), REPLICA, 0, 0, tiled=True)  7.62 us
  transfers between devices with their start and end apart: 18, of which 12 were waited for; matrix products, arithmetic and copies ran while one was open for 5% of the time, Pallas kernels for 11%

profile of v4, /device:TPU:1, one launch (start us, length us, event | category | flops | bytes accessed | tf_op | source)
XLA Modules:
  0.0 221.3 jit_solution(2999074595542309996)
XLA Ops:
  7.9 4.0 %collective-permute-start = (bf16[512,1536]{1,0:T(8,128)(2,1)}, bf16[512,1536]{1,0:T(8,128)(2,1)}, u32[]{:S(2)}, u32[]{:S(2)}) collective-permute-start(bf16[512,1536]{1,0:T(8,128)(2,1)} %param.6), channel_id=1, source_target_pairs={{0,32},{32,0},{1,33},{33,1},{2,34},{34,2},{3,35},{35,3},{4,36},{36... | collective-permute-start | bytes 4718600 | tf_op jit(solution)/shard_map/ppermute | solution.py:334
  12.0 6.7 %collective-permute-start.1 = (bf16[512,1536]{1,0:T(8,128)(2,1)}, bf16[512,1536]{1,0:T(8,128)(2,1)}, u32[]{:S(2)}, u32[]{:S(2)}) collective-permute-start(bf16[512,1536]{1,0:T(8,128)(2,1)} %param.6), channel_id=1, source_target_pairs={{0,16},{16,0},{1,17},{17,1},{2,18},{18,2},{3,19},{19,3},{4,20},{20... | collective-permute-start | bytes 4718600 | tf_op jit(solution)/shard_map/ppermute | solution.py:335
  18.7 1.9 collective-permute-start.3
  20.7 1.0 broadcast_in_dim.4
  21.6 4.2 %all-to-all-start = ((bf16[4,96,1024]{2,1,0:T(8,128)(2,1)}), bf16[4,96,1024]{2,1,0:T(8,128)(2,1)}, u32[]{:S(2)}, u32[]{:S(2)}) async-start(bf16[4,96,1024]{2,1,0:T(8,128)(2,1)} %broadcast_in_dim.4), calls=%async_computation | async-start | bytes 1572864 | tf_op jit(solution)/shard_map/all_to_all | solution.py:338
  25.9 1.1 resid_halves.1
  26.9 2.4 %collective-permute-start.2 = (bf16[32,1536]{1,0:T(8,128)(2,1)S(1)}, bf16[32,1536]{1,0:T(8,128)(2,1)S(1)}, u32[]{:S(2)}, u32[]{:S(2)}) collective-permute-start(bf16[32,1536]{1,0:T(8,128)(2,1)S(1)} %get-tuple-element.28), channel_id=1, source_target_pairs={{0,16},{16,0},{1,17},{17,1},{2,18},{18,2},{3,19},{19,3},{4,20},{20... | collective-permute-start | bytes 294920 | tf_op jit(solution)/shard_map/ppermute | solution.py:342
  29.4 0.9 collective-permute-done.2
  30.3 0.7 pad_maximum_fusion.resid
  31.0 1.0 norms.1
  32.0 1.3 copy-done.5
  33.9 3.8 %all-to-all-done = bf16[4,96,1024]{2,1,0:T(8,128)(2,1)} async-done(((bf16[4,96,1024]{2,1,0:T(8,128)(2,1)}), bf16[4,96,1024]{2,1,0:T(8,128)(2,1)}, u32[]{:S(2)}, u32[]{:S(2)}) %all-to-all-start) | async-done | bytes 786464 | tf_op jit(solution)/shard_map/all_to_all | solution.py:338
  37.8 3.7 %collective-permute-done = bf16[512,1536]{1,0:T(8,128)(2,1)} collective-permute-done((bf16[512,1536]{1,0:T(8,128)(2,1)}, bf16[512,1536]{1,0:T(8,128)(2,1)}, u32[]{:S(2)}, u32[]{:S(2)}) %collective-permute-start) | collective-permute-done | bytes 1572896 | tf_op jit(solution)/shard_map/ppermute | solution.py:334
  41.5 8.1 %collective-permute-start.4 = (bf16[512,1536]{1,0:T(8,128)(2,1)}, bf16[512,1536]{1,0:T(8,128)(2,1)S(1)}, u32[]{:S(2)}, u32[]{:S(2)}) collective-permute-start(bf16[512,1536]{1,0:T(8,128)(2,1)} %collective-permute-done), channel_id=1, source_target_pairs={{0,16},{16,0},{1,17},{17,1},{2,18},{18,2},{3,19},{19,3},{4,20},{20... | collective-permute-start | bytes 4718600 | tf_op jit(solution)/shard_map/ppermute | solution.py:347
  49.5 3.2 %collective-permute-done.4 = bf16[512,1536]{1,0:T(8,128)(2,1)S(1)} collective-permute-done((bf16[512,1536]{1,0:T(8,128)(2,1)}, bf16[512,1536]{1,0:T(8,128)(2,1)S(1)}, u32[]{:S(2)}, u32[]{:S(2)}) %collective-permute-start.4) | collective-permute-done | bytes 1572896 | tf_op jit(solution)/shard_map/ppermute | solution.py:347
  52.8 4.8 %all-gather.4.cloned.1.call-done = bf16[768,1536]{1,0:T(8,128)(2,1)} async-done(((bf16[96,1536]{1,0:T(8,128)(2,1)}), bf16[768,1536]{1,0:T(8,128)(2,1)}) %all-gather.4.cloned.1.call-update) | async-done | bytes 2359312 | tf_op jit(solution)/shard_map/all_gather | solution.py:332
  57.6 4.5 %product.3 = (bf16[1,4,2,32,768]{4,3,2,1,0:T(8,128)(2,1)}, bf16[1,4,2,32,768]{4,3,2,1,0:T(8,128)(2,1)}) custom-call(s32[1]{0:T(128)} %bitcast.16.owners, bf16[4,4,32,1536]{3,2,1,0:T(8,128)(2,1)} %bitcast.40, bf16[4,4,32,1536]{3,2,1,0:T(8,128)(2,1)} %bitcast.11.core, bf16[4,4,32,1536]{3,2,1,0:T(8,128)(2,1)} %bitcast.12.other, ...), custom_call_target="tpu_custom_call" | custom-call | flops 1207959552 | bytes 5000000 | tf_op jit(solution)/shard_map/product/pallas_call | solution.py:52
  62.1 3.1 %collective-permute-start.5 = (bf16[1,4,2,32,768]{4,3,2,1,0:T(8,128)(2,1)}, bf16[1,4,2,32,768]{4,3,2,1,0:T(8,128)(2,1)S(1)}, u32[]{:S(2)}, u32[]{:S(2)}) collective-permute-start(bf16[1,4,2,32,768]{4,3,2,1,0:T(8,128)(2,1)} %get-tuple-element.38), channel_id=1, source_target_pairs={{0,1},{1,2},{2,3},{3,0},{4,5},{5,6},{6,7},{7,4},{8,9},{9,10},{10,1... | collective-permute-start | bytes 1179656 | tf_op jit(solution)/shard_map/ppermute | solution.py:318
  65.2 3.4 %collective-permute-start.6 = (bf16[1,4,2,32,768]{4,3,2,1,0:T(8,128)(2,1)}, bf16[1,4,2,32,768]{4,3,2,1,0:T(8,128)(2,1)S(1)}, u32[]{:S(2)}, u32[]{:S(2)}) collective-permute-start(bf16[1,4,2,32,768]{4,3,2,1,0:T(8,128)(2,1)} %get-tuple-element.39), channel_id=1, source_target_pairs={{0,3},{1,0},{2,1},{3,2},{4,7},{5,4},{6,5},{7,6},{8,11},{9,8},{10,9... | collective-permute-start | bytes 1179656 | tf_op jit(solution)/shard_map/ppermute | solution.py:318
  69.2 11.3 %product.2 = (bf16[3,4,2,32,768]{4,3,2,1,0:T(8,128)(2,1)}, bf16[3,4,2,32,768]{4,3,2,1,0:T(8,128)(2,1)}) custom-call(s32[3]{0:T(128)} %pad_add_fusion.owners, bf16[4,4,32,1536]{3,2,1,0:T(8,128)(2,1)} %bitcast.41, bf16[4,4,32,1536]{3,2,1,0:T(8,128)(2,1)} %bitcast.11.core, bf16[4,4,32,1536]{3,2,1,0:T(8,128)(2,1)} %bitcast.12.other, ...), custom_call_target="tpu_custom_call" | custom-call | flops 3623878656 | bytes 15000000 | tf_op jit(solution)/shard_map/product/pallas_call | solution.py:52
  80.5 1.3 copy-done.1
  81.8 1.3 copy-done.3
  83.1 1.8 relay.1
  84.9 1.9 collective-permute-start.7
  86.8 4.6 %collective-permute-start.8 = (bf16[2,4,2,32,768]{4,3,2,1,0:T(8,128)(2,1)}, bf16[2,4,2,32,768]{4,3,2,1,0:T(8,128)(2,1)}, u32[]{:S(2)}, u32[]{:S(2)}) collective-permute-start(bf16[2,4,2,32,768]{4,3,2,1,0:T(8,128)(2,1)} %get-tuple-element.41), channel_id=1, source_target_pairs={{0,3},{1,0},{2,1},{3,2},{4,7},{5,4},{6,5},{7,6},{8,11},{9,8},{10,9... | collective-permute-start | bytes 2359304 | tf_op jit(solution)/shard_map/ppermute | solution.py:318
  91.4 11.5 %collective-permute-done.7.low = bf16[2,4,2,32,768]{4,3,2,1,0:T(8,128)(2,1)S(1)} collective-permute-done((bf16[2,4,2,32,768]{4,3,2,1,0:T(8,128)(2,1)}, bf16[2,4,2,32,768]{4,3,2,1,0:T(8,128)(2,1)S(1)}, u32[]{:S(2)}, u32[]{:S(2)}) %collective-permute-start.7) | collective-permute-done | bytes 786464 | tf_op jit(solution)/shard_map/ppermute | solution.py:318
  102.9 0.9 collective-permute-done.8.high
  103.8 3.4 %sum_x.1 = bf16[4,2,2,32,768]{4,3,2,1,0:T(8,128)(2,1)} custom-call(s32[1]{0:T(128)} %bitcast.yl, bf16[3,4,2,32,768]{4,3,2,1,0:T(8,128)(2,1)S(1)} %copy-done.2, bf16[3,4,2,32,768]{4,3,2,1,0:T(8,128)(2,1)S(1)} %copy-done.4, bf16[2,4,2,32,768]{4,3,2,1,0:T(8,128)(2,1)S(1)} %collective-permute-done.7.low, bf16[2,4,2,32,768]{4,3,2,1,0:T(8,128)(2,1)} %collective-permute-done.8.high), custom_call_target="tpu_custom_call" | custom-call | tf_op jit(solution)/shard_map/sum_x/pallas_call | solution.py:109
  107.2 6.7 %all-to-all-start.1 = ((bf16[8,64,768]{2,1,0:T(8,128)(2,1)}), bf16[8,64,768]{2,1,0:T(8,128)(2,1)S(1)}, u32[]{:S(2)}, u32[]{:S(2)}) async-start(bf16[8,64,768]{2,1,0:T(8,128)(2,1)} %bitcast.17), calls=%async_computation.1 | async-start | bytes 1572864 | tf_op jit(solution)/shard_map/all_to_all | solution.py:361
  113.9 28.2 %all-gather.6.cloned.1.call-done = bf16[16,96,1024]{2,1,0:T(8,128)(2,1)} async-done(((bf16[4,96,1024]{2,1,0:T(8,128)(2,1)}), bf16[16,96,1024]{2,1,0:T(8,128)(2,1)}) %all-gather.6.cloned.1.call-update) | async-done | bytes 3145744 | tf_op jit(solution)/shard_map/all_gather | solution.py:349
  142.2 3.9 %fusion.6.pred = f32[64,1536]{1,0:T(8,128)} fusion(bf16[64,1024]{1,0:T(8,128)(2,1)} %bitcast.34, bf16[1536,1024]{1,0:T(8,128)(2,1)} %bitcast.36), kind=kOutput, calls=%fused_computation.16 | convolution fusion | flops 201326592 | bytes 3670016 | tf_op jit(solution)/shard_map/dot_general | solution.py:26
  146.6 0.7 features.1
  147.3 6.8 %collective-permute-start.9 = (f32[2,64,128]{2,1,0:T(8,128)S(1)}, f32[2,64,128]{2,1,0:T(8,128)S(1)}, u32[]{:S(2)}, u32[]{:S(2)}) collective-permute-start(f32[2,64,128]{2,1,0:T(8,128)S(1)} %get-tuple-element.47.mine), channel_id=1, source_target_pairs={{0,16},{16,0},{1,17},{17,1},{2,18},{18,2},{3,19},{19,3},{4,20},{20... | collective-permute-start | bytes 196616 | tf_op jit(solution)/shard_map/ppermute | solution.py:366
  154.1 0.9 collective-permute-done.9.other
  155.0 1.0 copy-done.7
  156.3 17.2 %all_to_all.25 = bf16[16,64,96]{2,1,0:T(8,128)(2,1)S(1)} all-to-all(bf16[16,64,96]{2,1,0:T(8,128)(2,1)S(1)} %get-tuple-element.50), channel_id=1, replica_groups=mesh['z'=8,'yl'=2,'c'=2,'yh'=4,'x'=4] {'yh','x'}, dimensions={0} | all-to-all | bytes 393216 | tf_op jit(solution)/shard_map/all_to_all | solution.py:368
  173.4 1.4 grad_part.1
  174.9 9.4 %all-to-all-start.3 = ((bf16[16,48,128]{2,1,0:T(8,128)(2,1)}), bf16[16,48,128]{2,1,0:T(8,128)(2,1)S(1)}, u32[]{:S(2)}, u32[]{:S(2)}) async-start(bf16[16,48,128]{2,1,0:T(8,128)(2,1)} %grad_part.1), calls=%async_computation.3 | async-start | bytes 393216 | tf_op jit(solution)/shard_map/all_to_all | solution.py:370
  184.2 2.6 %fusion.7 = f32[64,1024]{1,0:T(8,128)S(1)} fusion(bf16[64,1536]{1,0:T(8,128)(2,1)S(1)} %get-tuple-element.49, bf16[1536,1024]{1,0:T(8,128)(2,1)} %bitcast.37), kind=kOutput, calls=%fused_computation.17 | convolution fusion | flops 201326592 | bytes 3604480 | tf_op jit(solution)/shard_map/dot_general | solution.py:374
  186.8 3.5 %collective-permute-start.10 = (bf16[32,1024]{1,0:T(8,128)(2,1)S(1)}, bf16[32,1024]{1,0:T(8,128)(2,1)S(1)}, u32[]{:S(2)}, u32[]{:S(2)}) collective-permute-start(bf16[32,1024]{1,0:T(8,128)(2,1)S(1)} %slice.19), channel_id=1, source_target_pairs={{0,16},{16,0},{1,17},{17,1},{2,18},{18,2},{3,19},{19,3},{4,20},{20... | collective-permute-start | bytes 196616 | tf_op jit(solution)/shard_map/ppermute | solution.py:375
  190.3 2.5 %all-to-all-done.3.got = bf16[16,48,128]{2,1,0:T(8,128)(2,1)S(1)} async-done(((bf16[16,48,128]{2,1,0:T(8,128)(2,1)}), bf16[16,48,128]{2,1,0:T(8,128)(2,1)S(1)}, u32[]{:S(2)}, u32[]{:S(2)}) %all-to-all-start.3) | async-done | bytes 196640 | tf_op jit(solution)/shard_map/all_to_all | solution.py:370
  192.8 0.7 sum_grad.1
  193.5 5.3 %all-to-all-start.4 = ((bf16[16,48,128]{2,1,0:T(8,128)(2,1)}), bf16[16,48,128]{2,1,0:T(8,128)(2,1)S(1)}, u32[]{:S(2)}, u32[]{:S(2)}) async-start(bf16[16,48,128]{2,1,0:T(8,128)(2,1)} %sum_grad.1), calls=%async_computation.4 | async-start | bytes 393216 | tf_op jit(solution)/shard_map/all_to_all | solution.py:371
  198.9 1.0 fusion.1
  199.9 7.6 %all-to-all-done.4.mine = bf16[16,48,128]{2,1,0:T(8,128)(2,1)S(1)} async-done(((bf16[16,48,128]{2,1,0:T(8,128)(2,1)}), bf16[16,48,128]{2,1,0:T(8,128)(2,1)S(1)}, u32[]{:S(2)}, u32[]{:S(2)}) %all-to-all-start.4) | async-done | bytes 196640 | tf_op jit(solution)/shard_map/all_to_all | solution.py:371
  207.5 4.5 %collective-permute-start.11 = (bf16[16,48,128]{2,1,0:T(8,128)(2,1)S(1)}, bf16[16,48,128]{2,1,0:T(8,128)(2,1)S(1)}, u32[]{:S(2)}, u32[]{:S(2)}) collective-permute-start(bf16[16,48,128]{2,1,0:T(8,128)(2,1)S(1)} %all-to-all-done.4.mine), channel_id=1, source_target_pairs={{0,16},{16,0},{1,17},{17,1},{2,18},{18,2},{3,19},{19,3},{4,20},{20... | collective-permute-start | bytes 589832 | tf_op jit(solution)/shard_map/ppermute | solution.py:372
  212.0 1.6 fusion.4
  213.6 0.9 join.1
  (40 shorter events, 2.9 us)
Async XLA Ops:
  7.2 13.4 %copy-start = (bf16[1024,192]{0,1:T(8,128)(2,1)S(1)}, bf16[1024,192]{0,1:T(8,128)(2,1)}, u32[]{:S(2)}) copy-start(bf16[1024,192]{0,1:T(8,128)(2,1)} %param.11) | copy-start | bytes 1179652
  7.2 23.8 %copy-start.8 = (bf16[512,1024]{1,0:T(8,128)(2,1)S(1)}, bf16[512,1024]{1,0:T(8,128)(2,1)}, u32[]{:S(2)}) copy-start(bf16[512,1024]{1,0:T(8,128)(2,1)} %param.9) | copy-start | bytes 3145732
  7.2 18.7 %copy-start.10 = (bf16[32,3072]{1,0:T(8,128)(2,1)S(1)}, bf16[32,3072]{1,0:T(8,128)(2,1)}, u32[]{:S(2)}) copy-start(bf16[32,3072]{1,0:T(8,128)(2,1)} %resid.1) | copy-start | bytes 589828
  7.2 23.8 %copy-start.12 = (f32[1024]{0:T(1024)S(1)}, f32[1024]{0:T(1024)}, u32[]{:S(2)}) copy-start(f32[1024]{0:T(1024)} %param.10) | copy-start | bytes 12292
  7.2 50.3 %all-gather.4.cloned.1.call-start = ((), (), s32[]{:S(2)}) async-start(), calls=%async_computation.5 | async-start | bytes 2654208 | tf_op jit(solution)/shard_map/all_gather | solution.py:332
  7.9 33.5 %collective-permute-start = (bf16[512,1536]{1,0:T(8,128)(2,1)}, bf16[512,1536]{1,0:T(8,128)(2,1)}, u32[]{:S(2)}, u32[]{:S(2)}) collective-permute-start(bf16[512,1536]{1,0:T(8,128)(2,1)} %param.6), channel_id=1, source_target_pairs={{0,32},{32,0},{1,33},{33,1},{2,34},{34,2},{3,35},{35,3},{4,36},{36... | collective-permute-start | bytes 4718600 | tf_op jit(solution)/shard_map/ppermute | solution.py:334
  12.0 29.5 %collective-permute-start.1 = (bf16[512,1536]{1,0:T(8,128)(2,1)}, bf16[512,1536]{1,0:T(8,128)(2,1)}, u32[]{:S(2)}, u32[]{:S(2)}) collective-permute-start(bf16[512,1536]{1,0:T(8,128)(2,1)} %param.6), channel_id=1, source_target_pairs={{0,16},{16,0},{1,17},{17,1},{2,18},{18,2},{3,19},{19,3},{4,20},{20... | collective-permute-start | bytes 4718600 | tf_op jit(solution)/shard_map/ppermute | solution.py:335
  18.7 12.3 %collective-permute-start.3 = (bf16[512,1024]{1,0:T(8,128)(2,1)}, bf16[512,1024]{1,0:T(8,128)(2,1)S(1)}, u32[]{:S(2)}, u32[]{:S(2)}) collective-permute-start(bf16[512,1024]{1,0:T(8,128)(2,1)} %param.9), channel_id=1, source_target_pairs={{0,16},{16,0},{1,17},{17,1},{2,18},{18,2},{3,19},{19,3},{4,20},{20... | collective-permute-start | bytes 3145736 | tf_op jit(solution)/shard_map/ppermute | solution.py:336
  21.6 16.1 %all-to-all-start = ((bf16[4,96,1024]{2,1,0:T(8,128)(2,1)}), bf16[4,96,1024]{2,1,0:T(8,128)(2,1)}, u32[]{:S(2)}, u32[]{:S(2)}) async-start(bf16[4,96,1024]{2,1,0:T(8,128)(2,1)} %broadcast_in_dim.4), calls=%async_computation | async-start | bytes 1572864 | tf_op jit(solution)/shard_map/all_to_all | solution.py:338
  25.8 116.3 %all-gather.6.cloned.1.call-start = ((), (), s32[]{:S(2)}) async-start(), calls=%async_computation.6 | async-start | bytes 3932160 | tf_op jit(solution)/shard_map/all_gather | solution.py:349
  26.9 3.3 %collective-permute-start.2 = (bf16[32,1536]{1,0:T(8,128)(2,1)S(1)}, bf16[32,1536]{1,0:T(8,128)(2,1)S(1)}, u32[]{:S(2)}, u32[]{:S(2)}) collective-permute-start(bf16[32,1536]{1,0:T(8,128)(2,1)S(1)} %get-tuple-element.28), channel_id=1, source_target_pairs={{0,16},{16,0},{1,17},{17,1},{2,18},{18,2},{3,19},{19,3},{4,20},{20... | collective-permute-start | bytes 294920 | tf_op jit(solution)/shard_map/ppermute | solution.py:342
  32.0 1.3 copy-start.5
  33.3 0.6 copy-start.11
  41.5 11.3 %collective-permute-start.4 = (bf16[512,1536]{1,0:T(8,128)(2,1)}, bf16[512,1536]{1,0:T(8,128)(2,1)S(1)}, u32[]{:S(2)}, u32[]{:S(2)}) collective-permute-start(bf16[512,1536]{1,0:T(8,128)(2,1)} %collective-permute-done), channel_id=1, source_target_pairs={{0,16},{16,0},{1,17},{17,1},{2,18},{18,2},{3,19},{19,3},{4,20},{20... | collective-permute-start | bytes 4718600 | tf_op jit(solution)/shard_map/ppermute | solution.py:347
  52.8 4.8 %copy-start.13 = (bf16[512,1536]{1,0:T(8,128)(2,1)}, bf16[512,1536]{1,0:T(8,128)(2,1)S(1)}, u32[]{:S(2)}) copy-start(bf16[512,1536]{1,0:T(8,128)(2,1)S(1)} %collective-permute-done.4) | copy-start | bytes 4718596
  62.1 18.4 %collective-permute-start.5 = (bf16[1,4,2,32,768]{4,3,2,1,0:T(8,128)(2,1)}, bf16[1,4,2,32,768]{4,3,2,1,0:T(8,128)(2,1)S(1)}, u32[]{:S(2)}, u32[]{:S(2)}) collective-permute-start(bf16[1,4,2,32,768]{4,3,2,1,0:T(8,128)(2,1)} %get-tuple-element.38), channel_id=1, source_target_pairs={{0,1},{1,2},{2,3},{3,0},{4,5},{5,6},{6,7},{7,4},{8,9},{9,10},{10,1... | collective-permute-start | bytes 1179656 | tf_op jit(solution)/shard_map/ppermute | solution.py:318
  65.2 15.3 %collective-permute-start.6 = (bf16[1,4,2,32,768]{4,3,2,1,0:T(8,128)(2,1)}, bf16[1,4,2,32,768]{4,3,2,1,0:T(8,128)(2,1)S(1)}, u32[]{:S(2)}, u32[]{:S(2)}) collective-permute-start(bf16[1,4,2,32,768]{4,3,2,1,0:T(8,128)(2,1)} %get-tuple-element.39), channel_id=1, source_target_pairs={{0,3},{1,0},{2,1},{3,2},{4,7},{5,4},{6,5},{7,6},{8,11},{9,8},{10,9... | collective-permute-start | bytes 1179656 | tf_op jit(solution)/shard_map/ppermute | solution.py:318
  80.5 1.3 copy-start.1
  81.8 1.3 copy-start.3
  83.1 20.7 %copy-start.2 = (bf16[3,4,2,32,768]{4,3,2,1,0:T(8,128)(2,1)S(1)}, bf16[3,4,2,32,768]{4,3,2,1,0:T(8,128)(2,1)}, u32[]{:S(2)}) copy-start(bf16[3,4,2,32,768]{4,3,2,1,0:T(8,128)(2,1)} %get-tuple-element.36.mine) | copy-start | bytes 3538948
  83.1 20.7 %copy-start.4 = (bf16[3,4,2,32,768]{4,3,2,1,0:T(8,128)(2,1)S(1)}, bf16[3,4,2,32,768]{4,3,2,1,0:T(8,128)(2,1)}, u32[]{:S(2)}) copy-start(bf16[3,4,2,32,768]{4,3,2,1,0:T(8,128)(2,1)} %get-tuple-element.37.rest) | copy-start | bytes 3538948
  84.9 18.0 %collective-permute-start.7 = (bf16[2,4,2,32,768]{4,3,2,1,0:T(8,128)(2,1)}, bf16[2,4,2,32,768]{4,3,2,1,0:T(8,128)(2,1)S(1)}, u32[]{:S(2)}, u32[]{:S(2)}) collective-permute-start(bf16[2,4,2,32,768]{4,3,2,1,0:T(8,128)(2,1)} %get-tuple-element.40), channel_id=1, source_target_pairs={{0,1},{1,2},{2,3},{3,0},{4,5},{5,6},{6,7},{7,4},{8,9},{9,10},{10,1... | collective-permute-start | bytes 2359304 | tf_op jit(solution)/shard_map/ppermute | solution.py:318
  86.8 17.0 %collective-permute-start.8 = (bf16[2,4,2,32,768]{4,3,2,1,0:T(8,128)(2,1)}, bf16[2,4,2,32,768]{4,3,2,1,0:T(8,128)(2,1)}, u32[]{:S(2)}, u32[]{:S(2)}) collective-permute-start(bf16[2,4,2,32,768]{4,3,2,1,0:T(8,128)(2,1)} %get-tuple-element.41), channel_id=1, source_target_pairs={{0,3},{1,0},{2,1},{3,2},{4,7},{5,4},{6,5},{7,6},{8,11},{9,8},{10,9... | collective-permute-start | bytes 2359304 | tf_op jit(solution)/shard_map/ppermute | solution.py:318
  107.2 39.4 %copy-start.9 = (bf16[64,1536]{1,0:T(8,128)(2,1)S(1)}, bf16[64,1536]{1,0:T(8,128)(2,1)}, u32[]{:S(2)}) copy-start(bf16[64,1536]{1,0:T(8,128)(2,1)} %pad_maximum_fusion.resid) | copy-start | bytes 589828
  107.2 39.4 %all-to-all-start.1 = ((bf16[8,64,768]{2,1,0:T(8,128)(2,1)}), bf16[8,64,768]{2,1,0:T(8,128)(2,1)S(1)}, u32[]{:S(2)}, u32[]{:S(2)}) async-start(bf16[8,64,768]{2,1,0:T(8,128)(2,1)} %bitcast.17), calls=%async_computation.1 | async-start | bytes 1572864 | tf_op jit(solution)/shard_map/all_to_all | solution.py:361
  142.2 31.3 %copy-start.6 = (bf16[16,2,32,1024]{3,2,1,0:T(8,128)(2,1)S(1)}, bf16[16,2,32,1024]{3,2,1,0:T(8,128)(2,1)}, u32[]{:S(2)}) copy-start(bf16[16,2,32,1024]{3,2,1,0:T(8,128)(2,1)} %copy-done.5) | copy-start | bytes 6291460
  147.3 7.7 %collective-permute-start.9 = (f32[2,64,128]{2,1,0:T(8,128)S(1)}, f32[2,64,128]{2,1,0:T(8,128)S(1)}, u32[]{:S(2)}, u32[]{:S(2)}) collective-permute-start(f32[2,64,128]{2,1,0:T(8,128)S(1)} %get-tuple-element.47.mine), channel_id=1, source_target_pairs={{0,16},{16,0},{1,17},{17,1},{2,18},{18,2},{3,19},{19,3},{4,20},{20... | collective-permute-start | bytes 196616 | tf_op jit(solution)/shard_map/ppermute | solution.py:366
  155.0 1.0 copy-start.7
  174.9 18.0 %all-to-all-start.3 = ((bf16[16,48,128]{2,1,0:T(8,128)(2,1)}), bf16[16,48,128]{2,1,0:T(8,128)(2,1)S(1)}, u32[]{:S(2)}, u32[]{:S(2)}) async-start(bf16[16,48,128]{2,1,0:T(8,128)(2,1)} %grad_part.1), calls=%async_computation.3 | async-start | bytes 393216 | tf_op jit(solution)/shard_map/all_to_all | solution.py:370
  186.8 12.1 %collective-permute-start.10 = (bf16[32,1024]{1,0:T(8,128)(2,1)S(1)}, bf16[32,1024]{1,0:T(8,128)(2,1)S(1)}, u32[]{:S(2)}, u32[]{:S(2)}) collective-permute-start(bf16[32,1024]{1,0:T(8,128)(2,1)S(1)} %slice.19), channel_id=1, source_target_pairs={{0,16},{16,0},{1,17},{17,1},{2,18},{18,2},{3,19},{19,3},{4,20},{20... | collective-permute-start | bytes 196616 | tf_op jit(solution)/shard_map/ppermute | solution.py:375
  193.5 14.0 %all-to-all-start.4 = ((bf16[16,48,128]{2,1,0:T(8,128)(2,1)}), bf16[16,48,128]{2,1,0:T(8,128)(2,1)S(1)}, u32[]{:S(2)}, u32[]{:S(2)}) async-start(bf16[16,48,128]{2,1,0:T(8,128)(2,1)} %sum_grad.1), calls=%async_computation.4 | async-start | bytes 393216 | tf_op jit(solution)/shard_map/all_to_all | solution.py:371
  207.5 6.1 %collective-permute-start.11 = (bf16[16,48,128]{2,1,0:T(8,128)(2,1)S(1)}, bf16[16,48,128]{2,1,0:T(8,128)(2,1)S(1)}, u32[]{:S(2)}, u32[]{:S(2)}) collective-permute-start(bf16[16,48,128]{2,1,0:T(8,128)(2,1)S(1)} %all-to-all-done.4.mine), channel_id=1, source_target_pairs={{0,16},{16,0},{1,17},{17,1},{2,18},{18,2},{3,19},{19,3},{4,20},{20... | collective-permute-start | bytes 589832 | tf_op jit(solution)/shard_map/ppermute | solution.py:372
Sparse Core Ops, SparseCore 0:
  10.1 47.3 all-gather.3
  59.6 82.4 all-gather.5
